TPU v7x, 256 devices: a whole 4x4x8 slice. The times are simulated.
256 devices in a mesh: pipe: 8 (over z_lo, y), dp: 32 (over x, z_hi, core).
Axes of the slice: x: 4, y: 4, z: 8 (z_hi: 4, z_lo: 2; z = z_hi * 2 + z_lo), core: 2. Of those that a mesh axis runs over, the one named last changes fastest.
Arguments:
- queries: bfloat16 [2, 8, 2048, 4096], P(None, 'pipe', 'dp'), may hold values from -5 to 5
- keys: bfloat16 [2, 8, 2048, 512], P(None, 'pipe', 'dp'), may hold values from -5 to 5
- values: bfloat16 [2, 8, 2048, 512], P(None, 'pipe', 'dp'), may hold values from -5 to 5
- out_grad: bfloat16 [2, 8, 2048, 4096], P(None, 'pipe', 'dp'), may hold values from -6 to 6
- block_input: bfloat16 [2, 8, 2048, 8192], P(None, 'pipe', 'dp'), may hold values from -64 to 64
- positions: int32 [2, 8, 2048], P(None, 'pipe', 'dp'), may hold values from 0 to 63, as said below
- direction: int32 [2], replicated, may hold values from 0 to 1, each once
- key_weight: bfloat16 [8, 8192, 512], P('pipe', 'dp'), may hold values from -0.1875 to 0.1875
- value_weight: bfloat16 [8, 8192, 512], P('pipe', 'dp'), may hold values from -0.1875 to 0.1875
- gain: bfloat16 [8, 8192], P('pipe', 'dp'), may hold values from 0.099609375 to 1.8984375
Outputs:
- query_grad: bfloat16 [2, 8, 2048, 4096], P(None, 'pipe', 'dp')
- passed_grad: bfloat16 [2, 8, 2048, 8192], P(None, 'pipe', 'dp')
- key_weight_grad: float32 [8, 8192, 512], P('pipe', 'dp')
- value_weight_grad: float32 [8, 8192, 512], P('pipe', 'dp')
- gain_grad: float32 [8, 8192], P('pipe', 'dp')
Inputs may be any that keep to these rules, and one draw needn't show every extreme that they name: `positions`: within every aligned block of 64 tokens the first position is 0, and each later position is the previous one plus 1 or else 0 where a new document starts. `direction`: the two entries are 0 and 1 in some order.
All inputs are finite; a program needn't handle non-finite values.
Results may differ from a plain program's by a relative error of at most 0.025.
Values may be sent and summed in bfloat16 or wider, within the bound.
A program may use at most 128 MiB of HBM per device.

v0:
```python
import jax
import jax.numpy as jnp
from jax import lax
from jax.sharding import PartitionSpec as P

KVH = 4
HD = 128
GROUP = 8
QW = 4096
KVW = 512


def from_behind(value, axis, steps):
    count = lax.axis_size(axis)
    first, last = (max(0, -steps), min(count, count - steps))
    return lax.ppermute(value, axis, [(source, source + steps) for source in range(first, last)])


def swapped_2(value, axis, stride):
    mask = 2**stride
    pairs = [(source, source ^ mask) for source in range(lax.axis_size(axis))]
    return lax.ppermute(value, axis, pairs)


def ordered(array, swapped):
    picked = array[:, 0]
    return jnp.where(swapped, picked[::-1], picked)


def attention_grads(queries, keys, values, out_grad, positions):
    batch = queries.shape[0]
    length = queries.shape[1]
    scale = HD ** (-0.5)
    query_heads = queries.reshape(batch, length, KVH, GROUP, HD)
    key_heads = keys.reshape(batch, length, KVH, HD)
    value_heads = values.reshape(batch, length, KVH, HD)
    grad_heads = out_grad.reshape(batch, length, KVH, GROUP, HD)
    scores = (
        jnp.einsum("bqkgd,bskd->bkgqs", query_heads, key_heads, preferred_element_type=jnp.float32)
        * scale
    )
    token_index = jnp.arange(length, dtype=jnp.int32)
    doc_start = token_index[None, :] - positions
    visible = (token_index[:, None] >= token_index[None, :])[None] & (
        doc_start[:, :, None] == doc_start[:, None, :]
    )
    scores = jnp.where(visible[:, None, None], scores, -1e30)
    top = jnp.max(scores, axis=-1, keepdims=True)
    weights = jnp.exp(scores - top)
    probs = weights / jnp.sum(weights, axis=-1, keepdims=True)
    probs_b = probs.astype(jnp.bfloat16)
    attn = jnp.einsum("bkgqs,bskd->bqkgd", probs_b, value_heads, preferred_element_type=jnp.float32)
    attn_b = attn.astype(jnp.bfloat16)
    delta = jnp.sum(grad_heads.astype(jnp.float32) * attn_b.astype(jnp.float32), axis=-1)
    delta = jnp.transpose(delta, (0, 2, 3, 1))
    dprobs = jnp.einsum(
        "bqkgd,bskd->bkgqs", grad_heads, value_heads, preferred_element_type=jnp.float32
    )
    dscore_b = (probs * (dprobs - delta[..., None])).astype(jnp.bfloat16)
    query_grad = jnp.einsum(
        "bkgqs,bskd->bqkgd", dscore_b, key_heads, preferred_element_type=jnp.float32
    )
    key_grad = jnp.einsum(
        "bkgqs,bqkgd->bskd", dscore_b, query_heads, preferred_element_type=jnp.float32
    )
    value_grad = jnp.einsum(
        "bkgqs,bqkgd->bskd", probs_b, grad_heads, preferred_element_type=jnp.float32
    )
    query_grad = (query_grad * scale).astype(jnp.bfloat16).reshape(batch, length, QW)
    key_grad = (key_grad * scale).astype(jnp.bfloat16).reshape(batch, length, KVW)
    value_grad = value_grad.astype(jnp.bfloat16).reshape(batch, length, KVW)
    return (query_grad, key_grad, value_grad)


def finish_rows(hidden_grad, column_inputs, gain_stack, scaled, inv_rms):
    gain_part = jnp.sum(hidden_grad * column_inputs.astype(jnp.float32), axis=1)
    column_grad = (hidden_grad * gain_stack[:, None, :]).astype(jnp.bfloat16)
    row_grad = lax.all_to_all(column_grad, "dp", split_axis=1, concat_axis=2, tiled=True).astype(
        jnp.float32
    )
    branch = inv_rms * (row_grad - scaled * jnp.mean(row_grad * scaled, axis=-1, keepdims=True))
    return (branch.astype(jnp.bfloat16), gain_part)


def send_sections(branch):
    from_after = from_behind(branch[0], "pipe", -1)
    from_before = from_behind(branch[1], "pipe", 1)
    return jnp.stack([from_after, from_before])


def bit_order(section_count):
    bit_list = list(range(section_count.bit_length() - 1))
    return bit_list


def on_device(
    queries,
    keys,
    values,
    out_grad,
    block_input,
    positions,
    direction,
    key_weight,
    value_weight,
    gain,
):
    swapped = direction[0] == 1
    query_rows = ordered(queries, swapped)
    key_rows = ordered(keys, swapped)
    value_rows = ordered(values, swapped)
    grad_rows = ordered(out_grad, swapped)
    input_rows = ordered(block_input, swapped)
    position_rows = ordered(positions, swapped)
    section_count = lax.axis_size("pipe")
    own_weights = jnp.concatenate([key_weight[0], value_weight[0]], axis=1)
    own_gain = gain[0]
    far_weights, far_gain = (own_weights, own_gain)
    for bit_index in bit_order(section_count):
        far_weights, far_gain = swapped_2((far_weights, far_gain), "pipe", bit_index)
    weight_stack = jnp.stack([own_weights, far_weights])
    gain_stack = jnp.stack([own_gain, far_gain]).astype(jnp.float32)
    inputs = input_rows.astype(jnp.float32)
    inv_rms = lax.rsqrt(jnp.mean(inputs * inputs, axis=-1, keepdims=True) + 1e-05)
    scaled = inputs * inv_rms
    normed = scaled.astype(jnp.bfloat16)
    query_grad, key_grad, value_grad = attention_grads(
        query_rows, key_rows, value_rows, grad_rows, position_rows
    )
    kv_grad = jnp.concatenate([key_grad, value_grad], axis=-1)
    column_inputs = lax.all_to_all(normed, "dp", split_axis=2, concat_axis=1, tiled=True)
    column_hidden = (column_inputs.astype(jnp.float32) * gain_stack[:, None, :]).astype(
        jnp.bfloat16
    )
    piece = lax.all_gather(kv_grad, "dp", axis=1, tiled=True)
    grad_part = jnp.einsum("tnc,trc->tnr", piece, weight_stack, preferred_element_type=jnp.float32)
    weight_acc = jnp.einsum(
        "tnr,tnc->trc", column_hidden, piece, preferred_element_type=jnp.float32
    )
    branch, gain_part = finish_rows(grad_part, column_inputs, gain_stack, scaled, inv_rms)
    passed = send_sections(branch)
    far_wgrad, far_ggrad = (weight_acc[1], gain_part[1])
    for bit_index in bit_order(section_count):
        far_wgrad, far_ggrad = swapped_2((far_wgrad, far_ggrad), "pipe", bit_index)
    total_weights = weight_acc[0] + far_wgrad
    total_gain = gain_part[0] + far_ggrad
    key_width = key_weight.shape[2]
    query_out = jnp.where(swapped, query_grad[::-1], query_grad)[:, None]
    passed_out = jnp.where(swapped, passed[::-1], passed)[:, None]
    return (
        query_out,
        passed_out,
        total_weights[None, :, :key_width],
        total_weights[None, :, key_width:],
        total_gain[None],
    )


def solution(mesh):
    in_specs = (
        P(None, "pipe", "dp", None),
        P(None, "pipe", "dp", None),
        P(None, "pipe", "dp", None),
        P(None, "pipe", "dp", None),
        P(None, "pipe", "dp", None),
        P(None, "pipe", "dp"),
        P(),
        P("pipe", "dp", None),
        P("pipe", "dp", None),
        P("pipe", "dp"),
    )
    out_specs = (
        P(None, "pipe", "dp", None),
        P(None, "pipe", "dp", None),
        P("pipe", "dp", None),
        P("pipe", "dp", None),
        P("pipe", "dp"),
    )
    return jax.shard_map(
        on_device, mesh=mesh, in_specs=in_specs, out_specs=out_specs, check_vma=False
    )
```

profile of v0, /device:TPU:30, one launch (start us, length us, event | category | flops | bytes accessed | tf_op | source)
XLA Modules:
  0.0 325.9 jit_solution(5355557848348984765)
XLA Ops:
  10.5 3.0 reverse_select_fusion.3
  14.2 2.8 fusion.58
  16.9 1.9 fusion.36
  21.2 2.4 fusion.14
  25.1 2.2 fusion.20
  28.9 1.9 fusion.1
  30.7 9.5 %copy.87 = bf16[2,64,8192]{1,0,2:T(2,128)(2,1)} copy(bf16[2,64,8192]{2,1,0:T(8,128)(2,1)} %fusion.1) | data formatting | bytes 4194304 | tf_op jit(solution)/shard_map/convert_element_type | solution.py:126
  40.2 9.8 %reshape.106 = bf16[32,2,16384]{2,1,0:T(2,128)(2,1)} reshape(bf16[8192,2,64]{2,1,0:T(2,128)(2,1)} %bitcast.133) | data formatting | bytes 4194304
  50.1 11.8 %all-to-all-start.1 = ((bf16[32,2,16384]{2,1,0:T(2,128)(2,1)}), bf16[32,2,16384]{2,1,0:T(2,128)(2,1)}, u32[]{:S(2)}, u32[]{:S(2)}) async-start(bf16[32,2,16384]{2,1,0:T(2,128)(2,1)} %reshape.106), calls=%async_computation.1 | async-start | bytes 4194304 | tf_op jit(solution)/shard_map/all_to_all | solution.py:131
  61.9 1.9 fusion.56
  64.5 13.2 %collective-permute-done = bf16[256,1024]{1,0:T(8,128)(2,1)S(1)} collective-permute-done((bf16[256,1024]{1,0:T(8,128)(2,1)S(1)}, bf16[256,1024]{1,0:T(8,128)(2,1)S(1)}, u32[]{:S(2)}, u32[]{:S(2)}) %collective-permute-start) | collective-permute-done | bytes 524320 | tf_op jit(solution)/shard_map/ppermute | solution.py:22
  79.0 13.6 %collective-permute-done.1 = bf16[256,1024]{1,0:T(8,128)(2,1)} collective-permute-done((bf16[256,1024]{1,0:T(8,128)(2,1)S(1)}, bf16[256,1024]{1,0:T(8,128)(2,1)}, u32[]{:S(2)}, u32[]{:S(2)}) %collective-permute-start.1) | collective-permute-done | bytes 524320 | tf_op jit(solution)/shard_map/ppermute | solution.py:22
  94.5 2.8 collective-permute-done.3
  98.5 3.8 %collective-permute-done.4 = bf16[256]{0:T(256)(128)(2,1)S(1)} collective-permute-done((bf16[256]{0:T(256)(128)(2,1)S(1)}, bf16[256]{0:T(256)(128)(2,1)S(1)}, u32[]{:S(2)}, u32[]{:S(2)}) %collective-permute-start.4) | collective-permute-done | bytes 544 | tf_op jit(solution)/shard_map/ppermute | solution.py:22
  103.3 50.6 %collective-permute-done.5 = bf16[256]{0:T(256)(128)(2,1)S(1)} collective-permute-done((bf16[256]{0:T(256)(128)(2,1)S(1)}, bf16[256]{0:T(256)(128)(2,1)S(1)}, u32[]{:S(2)}, u32[]{:S(2)}) %collective-permute-start.5) | collective-permute-done | bytes 544 | tf_op jit(solution)/shard_map/ppermute | solution.py:22
  154.0 9.8 %reshape.107 = bf16[8192,2,64]{2,1,0:T(2,128)(2,1)} reshape(bf16[32,2,16384]{2,1,0:T(2,128)(2,1)} %all-to-all-done.1) | data formatting | bytes 4194304
  163.8 10.6 %copy.88 = f32[2,64,32,256]{3,1,2,0:T(8,128)} copy(bf16[2,64,32,256]{1,0,3,2:T(2,128)(2,1)} %bitcast.134) | data formatting | bytes 6291456 | tf_op jit(solution)/shard_map/convert_element_type | solution.py:132
  174.3 9.1 %fusion.10 = (f32[2,256]{1,0:T(2,128)S(1)}, bf16[2,2048,256]{2,1,0:T(8,128)(2,1)}, bf16[2,2048,256]{2,1,0:T(8,128)(2,1)S(1)}) fusion(f32[2,64,32,256]{3,1,2,0:T(8,128)} %copy.88, f32[2,256]{1,0:T(2,128)S(1)} %maximum_convert_fusion, bf16[2,2048,1024]{2,1,0:T(8,128)(2,1)} %all-gather.2.cloned.1.call-done, bf16[1,256,1024]{2,1,0:T(8,128)(2,1)} %bitcast.27, ...), kind=kOutput, calls=%fused_computation.14 | convolution fusion | flops 2154298880 | bytes 17829888 | tf_op jit(solution)/shard_map/tnc,trc->tnr/dot_general | solution.py:136
  183.4 14.0 %copy.85 = bf16[2,2048,256]{2,0,1:T(2,128)(2,1)} copy(bf16[2,2048,256]{2,1,0:T(8,128)(2,1)S(1)} %get-tuple-element.22) | data formatting | bytes 4194304 | tf_op jit(solution)/shard_map/convert_element_type | solution.py:77
  197.4 9.4 %all-to-all-start = ((bf16[2,2048,256]{2,0,1:T(2,128)(2,1)}), bf16[2,2048,256]{2,0,1:T(2,128)(2,1)}, u32[]{:S(2)}, u32[]{:S(2)}) async-start(bf16[2,2048,256]{2,0,1:T(2,128)(2,1)} %copy.85), calls=%async_computation | async-start | bytes 4194304 | tf_op jit(solution)/shard_map/all_to_all | solution.py:78
  206.8 6.4 %fusion.63 = f32[2,256,1024]{2,1,0:T(8,128)S(1)} fusion(bf16[2,2048,256]{2,1,0:T(8,128)(2,1)} %get-tuple-element.21, bf16[2,2048,1024]{2,1,0:T(8,128)(2,1)} %all-gather.2.cloned.1.call-done), kind=kOutput, calls=%fused_computation.86 | convolution fusion | flops 2147483648 | bytes 12582912 | tf_op jit(solution)/shard_map/tnr,tnc->trc/dot_general | solution.py:137
  214.1 24.6 %collective-permute-done.8 = f32[256,1024]{1,0:T(8,128)} collective-permute-done((f32[256,1024]{1,0:T(8,128)S(1)}, f32[256,1024]{1,0:T(8,128)}, u32[]{:S(2)}, u32[]{:S(2)}) %collective-permute-start.8) | collective-permute-done | bytes 1048608 | tf_op jit(solution)/shard_map/ppermute | solution.py:22
  239.9 22.4 %collective-permute-done.11 = f32[256]{0:T(256)S(1)} collective-permute-done((f32[256]{0:T(256)S(1)}, f32[256]{0:T(256)S(1)}, u32[]{:S(2)}, u32[]{:S(2)}) %collective-permute-start.11) | collective-permute-done | bytes 1056 | tf_op jit(solution)/shard_map/ppermute | solution.py:22
  262.3 3.8 %collective-permute-start.12 = (f32[256]{0:T(256)S(1)}, f32[256]{0:T(256)S(1)}, u32[]{:S(2)}, u32[]{:S(2)}) collective-permute-start(f32[256]{0:T(256)S(1)} %collective-permute-done.11), channel_id=1, source_target_pairs={{0,64},{32,96},{64,0},{96,32},{128,192},{160,224},{192,128},{224,1... | collective-permute-start | bytes 3080 | tf_op jit(solution)/shard_map/ppermute | solution.py:22
  266.6 1.6 copy.78
  271.9 4.8 %copy.149 = f32[2,32,64,256]{3,1,2,0:T(8,128)} copy(bf16[2,32,64,256]{3,0,2,1:T(2,128)(2,1)} %bitcast.48) | data formatting | bytes 6291456 | tf_op jit(solution)/shard_map/convert_element_type | solution.py:78
  276.7 5.0 %reshape.95 = f32[2,64,8192]{2,1,0:T(8,128)} reshape(f32[2,64,32,256]{3,2,1,0:T(8,128)} %bitcast.135) | data formatting | bytes 8388608 | tf_op jit(solution)/shard_map/convert_element_type | solution.py:78
  281.7 3.2 fusion.4
  286.3 2.2 collective-permute-start.6
  288.5 5.9 %collective-permute-start.7 = (bf16[64,8192]{1,0:T(8,128)(2,1)S(1)}, bf16[64,8192]{1,0:T(8,128)(2,1)S(1)}, u32[]{:S(2)}, u32[]{:S(2)}) collective-permute-start(bf16[64,8192]{1,0:T(8,128)(2,1)S(1)} %get-tuple-element.24), channel_id=1, source_target_pairs={{0,32},{32,64},{64,96},{96,128},{128,160},{160,192},{192,224},{1,3... | collective-permute-start | bytes 3145736 | tf_op jit(solution)/shard_map/ppermute | solution.py:16
  298.6 18.5 %collective-permute-done.6 = bf16[64,8192]{1,0:T(8,128)(2,1)S(1)} collective-permute-done((bf16[64,8192]{1,0:T(8,128)(2,1)S(1)}, bf16[64,8192]{1,0:T(8,128)(2,1)S(1)}, u32[]{:S(2)}, u32[]{:S(2)}) %collective-permute-start.6) | collective-permute-done | bytes 1048608 | tf_op jit(solution)/shard_map/ppermute | solution.py:16
  317.3 1.7 fusion.11
  (77 shorter events, 26.6 us)
Async XLA Ops:
  7.2 167.2 %all-gather.2.cloned.1.call-start = ((), (), s32[]{:S(2)}) async-start(), calls=%async_computation.2 | async-start | bytes 8650752 | tf_op jit(solution)/shard_map/all_gather | solution.py:135
  13.8 6.8 %copy-start.5 = (bf16[16,8,32,128]{3,2,1,0:T(8,128)(2,1)}, bf16[16,8,32,128]{3,2,1,0:T(8,128)(2,1)S(1)}, u32[]{:S(2)}) copy-start(bf16[16,8,32,128]{3,2,1,0:T(8,128)(2,1)S(1)} %copy.112) | copy-start | bytes 3145732
  14.1 2.9 copy-start.4
  16.9 2.7 copy-start.8
  19.6 1.6 copy-start.6
  19.6 1.6 copy-start.9
  25.1 3.0 copy-start.1
  50.0 11.8 %copy-start.7 = (bf16[1,256,512]{2,1,0:T(8,128)(2,1)S(1)}, bf16[1,256,512]{2,1,0:T(8,128)(2,1)}, u32[]{:S(2)}) copy-start(bf16[1,256,512]{2,1,0:T(8,128)(2,1)} %param.18) | copy-start | bytes 786436
  50.0 43.6 %copy-start.10 = (bf16[1,256]{1,0:T(2,128)(2,1)S(1)}, bf16[1,256]{1,0:T(2,128)(2,1)}, u32[]{:S(2)}) copy-start(bf16[1,256]{1,0:T(2,128)(2,1)} %param.19) | copy-start | bytes 1540
  50.1 103.9 %all-to-all-start.1 = ((bf16[32,2,16384]{2,1,0:T(2,128)(2,1)}), bf16[32,2,16384]{2,1,0:T(2,128)(2,1)}, u32[]{:S(2)}, u32[]{:S(2)}) async-start(bf16[32,2,16384]{2,1,0:T(2,128)(2,1)} %reshape.106), calls=%async_computation.1 | async-start | bytes 4194304 | tf_op jit(solution)/shard_map/all_to_all | solution.py:131
  63.8 14.0 %collective-permute-start = (bf16[256,1024]{1,0:T(8,128)(2,1)S(1)}, bf16[256,1024]{1,0:T(8,128)(2,1)S(1)}, u32[]{:S(2)}, u32[]{:S(2)}) collective-permute-start(bf16[256,1024]{1,0:T(8,128)(2,1)S(1)} %get-tuple-element.28), channel_id=1, source_target_pairs={{0,32},{32,0},{64,96},{96,64},{128,160},{160,128},{192,224},{224,1... | collective-permute-start | bytes 1572872 | tf_op jit(solution)/shard_map/ppermute | solution.py:22
  77.7 14.9 %collective-permute-start.1 = (bf16[256,1024]{1,0:T(8,128)(2,1)S(1)}, bf16[256,1024]{1,0:T(8,128)(2,1)}, u32[]{:S(2)}, u32[]{:S(2)}) collective-permute-start(bf16[256,1024]{1,0:T(8,128)(2,1)S(1)} %collective-permute-done), channel_id=1, source_target_pairs={{0,64},{32,96},{64,0},{96,32},{128,192},{160,224},{192,128},{224,1... | collective-permute-start | bytes 1572872 | tf_op jit(solution)/shard_map/ppermute | solution.py:22
  92.6 81.7 %collective-permute-start.2 = (bf16[256,1024]{1,0:T(8,128)(2,1)}, bf16[256,1024]{1,0:T(8,128)(2,1)}, u32[]{:S(2)}, u32[]{:S(2)}) collective-permute-start(bf16[256,1024]{1,0:T(8,128)(2,1)} %collective-permute-done.1), channel_id=1, source_target_pairs={{0,128},{32,160},{64,192},{96,224},{128,0},{160,32},{192,64},{224,... | collective-permute-start | bytes 1572872 | tf_op jit(solution)/shard_map/ppermute | solution.py:22
  93.6 3.6 %collective-permute-start.3 = (bf16[256]{0:T(256)(128)(2,1)S(1)}, bf16[256]{0:T(256)(128)(2,1)S(1)}, u32[]{:S(2)}, u32[]{:S(2)}) collective-permute-start(bf16[256]{0:T(256)(128)(2,1)S(1)} %reduce), channel_id=1, source_target_pairs={{0,32},{32,0},{64,96},{96,64},{128,160},{160,128},{192,224},{224,1... | collective-permute-start | bytes 1544 | tf_op jit(solution)/shard_map/ppermute | solution.py:22
  97.3 5.0 %collective-permute-start.4 = (bf16[256]{0:T(256)(128)(2,1)S(1)}, bf16[256]{0:T(256)(128)(2,1)S(1)}, u32[]{:S(2)}, u32[]{:S(2)}) collective-permute-start(bf16[256]{0:T(256)(128)(2,1)S(1)} %collective-permute-done.3), channel_id=1, source_target_pairs={{0,64},{32,96},{64,0},{96,32},{128,192},{160,224},{192,128},{224,1... | collective-permute-start | bytes 1544 | tf_op jit(solution)/shard_map/ppermute | solution.py:22
  102.3 51.7 %collective-permute-start.5 = (bf16[256]{0:T(256)(128)(2,1)S(1)}, bf16[256]{0:T(256)(128)(2,1)S(1)}, u32[]{:S(2)}, u32[]{:S(2)}) collective-permute-start(bf16[256]{0:T(256)(128)(2,1)S(1)} %collective-permute-done.4), channel_id=1, source_target_pairs={{0,128},{32,160},{64,192},{96,224},{128,0},{160,32},{192,64},{224,... | collective-permute-start | bytes 1544 | tf_op jit(solution)/shard_map/ppermute | solution.py:22
  197.4 74.6 %all-to-all-start = ((bf16[2,2048,256]{2,0,1:T(2,128)(2,1)}), bf16[2,2048,256]{2,0,1:T(2,128)(2,1)}, u32[]{:S(2)}, u32[]{:S(2)}) async-start(bf16[2,2048,256]{2,0,1:T(2,128)(2,1)} %copy.85), calls=%async_computation | async-start | bytes 4194304 | tf_op jit(solution)/shard_map/all_to_all | solution.py:78
  213.2 53.4 %copy-start.2 = (f32[2,256,1024]{2,1,0:T(8,128)}, f32[2,256,1024]{2,1,0:T(8,128)S(1)}, u32[]{:S(2)}) copy-start(f32[2,256,1024]{2,1,0:T(8,128)S(1)} %fusion.63) | copy-start | bytes 6291460
  213.3 25.4 %collective-permute-start.8 = (f32[256,1024]{1,0:T(8,128)S(1)}, f32[256,1024]{1,0:T(8,128)}, u32[]{:S(2)}, u32[]{:S(2)}) collective-permute-start(f32[256,1024]{1,0:T(8,128)S(1)} %slice_bitcast_fusion), channel_id=1, source_target_pairs={{0,32},{32,0},{64,96},{96,64},{128,160},{160,128},{192,224},{224,1... | collective-permute-start | bytes 3145736 | tf_op jit(solution)/shard_map/ppermute | solution.py:22
  238.7 32.3 %collective-permute-start.9 = (f32[256,1024]{1,0:T(8,128)}, f32[256,1024]{1,0:T(8,128)}, u32[]{:S(2)}, u32[]{:S(2)}) collective-permute-start(f32[256,1024]{1,0:T(8,128)} %collective-permute-done.8), channel_id=1, source_target_pairs={{0,64},{32,96},{64,0},{96,32},{128,192},{160,224},{192,128},{224,1... | collective-permute-start | bytes 3145736 | tf_op jit(solution)/shard_map/ppermute | solution.py:22
  239.9 22.4 %collective-permute-start.11 = (f32[256]{0:T(256)S(1)}, f32[256]{0:T(256)S(1)}, u32[]{:S(2)}, u32[]{:S(2)}) collective-permute-start(f32[256]{0:T(256)S(1)} %bitcast.161), channel_id=1, source_target_pairs={{0,32},{32,0},{64,96},{96,64},{128,160},{160,128},{192,224},{224,1... | collective-permute-start | bytes 3080 | tf_op jit(solution)/shard_map/ppermute | solution.py:22
  262.3 7.5 %collective-permute-start.12 = (f32[256]{0:T(256)S(1)}, f32[256]{0:T(256)S(1)}, u32[]{:S(2)}, u32[]{:S(2)}) collective-permute-start(f32[256]{0:T(256)S(1)} %collective-permute-done.11), channel_id=1, source_target_pairs={{0,64},{32,96},{64,0},{96,32},{128,192},{160,224},{192,128},{224,1... | collective-permute-start | bytes 3080 | tf_op jit(solution)/shard_map/ppermute | solution.py:22
  269.8 25.8 %collective-permute-start.13 = (f32[256]{0:T(256)S(1)}, f32[256]{0:T(256)S(1)}, u32[]{:S(2)}, u32[]{:S(2)}) collective-permute-start(f32[256]{0:T(256)S(1)} %collective-permute-done.12), channel_id=1, source_target_pairs={{0,128},{32,160},{64,192},{96,224},{128,0},{160,32},{192,64},{224,... | collective-permute-start | bytes 3080 | tf_op jit(solution)/shard_map/ppermute | solution.py:22
  271.0 25.2 %collective-permute-start.10 = (f32[256,1024]{1,0:T(8,128)}, f32[256,1024]{1,0:T(8,128)}, u32[]{:S(2)}, u32[]{:S(2)}) collective-permute-start(f32[256,1024]{1,0:T(8,128)} %collective-permute-done.9), channel_id=1, source_target_pairs={{0,128},{32,160},{64,192},{96,224},{128,0},{160,32},{192,64},{224,... | collective-permute-start | bytes 3145736 | tf_op jit(solution)/shard_map/ppermute | solution.py:22
  281.7 3.4 %copy-start = (f32[2,64,8192]{2,1,0:T(8,128)S(1)}, f32[2,64,8192]{2,1,0:T(8,128)}, u32[]{:S(2)}) copy-start(f32[2,64,8192]{2,1,0:T(8,128)} %reshape.95) | copy-start | bytes 12582916
  286.3 9.8 %copy-start.3 = (f32[2,256,1024]{2,1,0:T(8,128)S(1)}, f32[2,256,1024]{2,1,0:T(8,128)}, u32[]{:S(2)}) copy-start(f32[2,256,1024]{2,1,0:T(8,128)} %copy-done.2) | copy-start | bytes 6291460
  286.3 30.8 %collective-permute-start.6 = (bf16[64,8192]{1,0:T(8,128)(2,1)S(1)}, bf16[64,8192]{1,0:T(8,128)(2,1)S(1)}, u32[]{:S(2)}, u32[]{:S(2)}) collective-permute-start(bf16[64,8192]{1,0:T(8,128)(2,1)S(1)} %get-tuple-element.23), channel_id=1, source_target_pairs={{32,0},{64,32},{96,64},{128,96},{160,128},{192,160},{224,192},{33,... | collective-permute-start | bytes 3145736 | tf_op jit(solution)/shard_map/ppermute | solution.py:16
  288.5 28.6 %collective-permute-start.7 = (bf16[64,8192]{1,0:T(8,128)(2,1)S(1)}, bf16[64,8192]{1,0:T(8,128)(2,1)S(1)}, u32[]{:S(2)}, u32[]{:S(2)}) collective-permute-start(bf16[64,8192]{1,0:T(8,128)(2,1)S(1)} %get-tuple-element.24), channel_id=1, source_target_pairs={{0,32},{32,64},{64,96},{96,128},{128,160},{160,192},{192,224},{1,3... | collective-permute-start | bytes 3145736 | tf_op jit(solution)/shard_map/ppermute | solution.py:16
Sparse Core Ops, SparseCore 0:
  28.1 124.0 all-gather.1
where the time goes:
time: 328 us; the launch traced here: 326 us
  waiting for transfers between devices  150 us (46%)
  local copies, waits for them, and re-layouts  71.7 us (22%)
  starting transfers between devices  43.3 us (13%)
  matrix products  24.8 us (8%)
  other arithmetic  21.4 us (7%)
  between operations  15 us (5%)
    ppermute x12, waiting for transfers between devices, swapped_2(): return lax.ppermute(value, axis, pairs)  131 us
    unnamed x26, local copies, waits for them, and re-layouts  20.4 us
    ppermute x2, waiting for transfers between devices, from_behind(): lax.ppermute(value, axis, [(source, source + steps) for source in range(f...  18.5 us
    convert_element_type x1, local copies, waits for them, and re-layouts, finish_rows(): column_grad = (hidden_grad * gain_stack[:, None, :]).astype(jnp.bfloat16)  14 us
    ppermute x12, starting transfers between devices, swapped_2(): return lax.ppermute(value, axis, pairs)  13.9 us
    all_to_all x1, starting transfers between devices, on_device(): lax.all_to_all(normed, 'dp', split_axis=2, concat_axis=1, tiled=True)  11.8 us
    convert_element_type x1, local copies, waits for them, and re-layouts, on_device(): column_inputs.astype(jnp.float32) * gain_stack[:, None, :]  10.6 us
    convert_element_type x2, local copies, waits for them, and re-layouts, finish_rows(): lax.all_to_all(column_grad, 'dp', split_axis=1, concat_axis=2, tiled=True)  9.76 us
  transfers between devices with their start and end apart: 17, of which 8 were waited for; matrix products, arithmetic and copies ran while one was open for 22% of the time, Pallas kernels for 0%

commit v1 on v0

v1 whole, which is shorter than its diff:
```python
import functools

import jax
import jax.numpy as jnp
from jax import lax
from jax.experimental import pallas as pl
from jax.experimental.pallas import tpu as pltpu
from jax.sharding import PartitionSpec as P

KVH = 4
HD = 128
GROUP = 8
SEQ = 64
QW = 4096
KVW = 512
D = 8192
BLK = 256
KW = 2 * KVW
KX = KW + 128
HALF = BLK // 2
MESH = pl.DeviceIdType.MESH
F32 = jnp.float32
BF16 = jnp.bfloat16


def dot(a, b, ca, cb):
    return lax.dot_general(a, b, (((ca,), (cb,)), ((), ())), preferred_element_type=F32)


def kernel(
    flag,
    pos,
    keys,
    values,
    gain,
    q_hbm,
    og_hbm,
    inp_hbm,
    kw_hbm,
    vw_hbm,
    qg_out,
    passed_out,
    wk_out,
    wv_out,
    gg_out,
    q,
    og,
    inp,
    nsend,
    nrecv,
    invs,
    vis,
    kvm,
    kvsnd,
    kvall,
    wall,
    gall,
    hbuf,
    part,
    rsf_s,
    rsf_r,
    rsn_s,
    rsn_r,
    ngb,
    cacc,
    gpart,
    gg_r,
    c_s,
    c_r,
    cbuf,
    bsend,
    brecv,
    lsem,
    ns_s,
    ns_r,
    g_s,
    g_r,
    km_s,
    km_r,
    kx_s,
    kx_r,
    kc_s,
    kc_r,
    w_s,
    w_r,
    rs_s,
    rs_r,
    gg_ss,
    gg_rs,
    c_ss,
    c_rs,
    b_s,
    b_r,
):
    p = lax.axis_index("pipe")
    d = lax.axis_index("dp")
    zl = lax.div(p, 4)
    x = lax.div(d, 8)
    zh = lax.rem(lax.div(d, 2), 4)
    c = lax.rem(d, 2)
    slot = x * 2 + c
    zp = lax.rem(zh + 1, 4)
    zf = lax.rem(zh + 2, 4)
    zm = lax.rem(zh + 3, 4)

    def dev(pp, xx, zz, cc):
        return (pp, xx * 8 + zz * 2 + cc)

    def mir(cc):
        return lax.rem(zh + 4 + cc * (2 * zl - 1), 4)

    def remote(src, dst, ss, rs, to):
        return pltpu.make_async_remote_copy(
            src_ref=src, dst_ref=dst, send_sem=ss, recv_sem=rs, device_id=to, device_id_type=MESH
        )

    def here(ss, rs, ref):
        return remote(ref, ref, ss, rs, dev(p, x, zh, 1 - c))

    def loop(lo, hi, f):
        def step(i, carry):
            f(i)
            return carry

        lax.fori_loop(lo, hi, step, 0)

    load_inp = pltpu.make_async_copy(inp_hbm, inp, lsem.at[0])
    load_kw = pltpu.make_async_copy(kw_hbm, wall.at[zh, :, pl.ds(0, KVW)], lsem.at[1])
    load_vw = pltpu.make_async_copy(vw_hbm, wall.at[zh, :, pl.ds(KVW, KVW)], lsem.at[2])
    load_q = pltpu.make_async_copy(q_hbm, q, lsem.at[3])
    load_og = pltpu.make_async_copy(og_hbm, og, lsem.at[4])
    load_kw.start()
    load_vw.start()
    load_inp.start()
    load_q.start()
    load_og.start()

    bar = pltpu.get_barrier_semaphore()

    def greet(to):
        pl.semaphore_signal(bar, inc=1, device_id=to, device_id_type=MESH)

    back_up = p >= 1
    back_down = p <= 6
    self_up = jnp.logical_and(p == 4, c == 0)
    zlm = lax.div(p + 3, 4) - 1
    zup = lax.rem(zh + 4 + c * (2 * zlm - 1), 4)

    for zz in (zp, zm, zf):
        greet(dev(p, x, zz, c))

    def greet_all(j):
        t = lax.rem(slot + j, 8)
        xx = lax.div(t, 2)
        cc = lax.rem(t, 2)

        @pl.when(j > 0)
        def _():
            greet(dev(p, xx, zh, cc))

        greet(dev(7 - p, xx, mir(cc), cc))

        @pl.when(back_down)
        def _():
            greet(dev(p + 1, xx, zh, cc))

        @pl.when(jnp.logical_and(back_up, jnp.logical_not(jnp.logical_and(self_up, j == 0))))
        def _():
            greet(dev(8 - p, xx, zup, cc))

    loop(0, 8, greet_all)
    gall[zh] = jnp.broadcast_to(gain[...], (16, BLK))
    n_back = jnp.where(back_up, 16, 0) - jnp.where(self_up, 1, 0)
    pl.semaphore_wait(bar, 18 + n_back)

    for j, zz in ((1, zp), (2, zf), (3, zm)):
        remote(gall.at[zh], gall.at[zh], g_s.at[j], g_r.at[j], dev(p, x, zz, c)).start()
    load_kw.wait()
    load_vw.wait()
    remote(wall.at[zh], wall.at[zh], w_s.at[0], w_r.at[0], dev(p, x, zp, c)).start()
    remote(wall.at[zh], wall.at[zh], w_s.at[1], w_r.at[1], dev(p, x, zm, c)).start()

    swap = flag[0] == 1
    load_inp.wait()

    def norm_rows(i):
        r = pl.ds(pl.multiple_of(i * 16, 16), 16)
        sq = [jnp.zeros((16, BLK), F32), jnp.zeros((16, BLK), F32)]
        for j in range(32):
            for m in range(2):
                v = inp[m, r, j * BLK : (j + 1) * BLK].astype(F32)
                sq[m] = sq[m] + v * v
        inv = [lax.rsqrt(jnp.sum(s, axis=1, keepdims=True) * (1.0 / D) + 1e-05) for s in sq]
        for j in range(32):
            t = (j // 8) * 2 + j % 2
            b = (j // 2) % 4
            v0 = inp[0, r, j * BLK : (j + 1) * BLK].astype(F32) * inv[0]
            v1 = inp[1, r, j * BLK : (j + 1) * BLK].astype(F32) * inv[1]
            nsend[0, t, b, r, :] = jnp.where(swap, v1, v0).astype(BF16)
            nsend[1, t, b, r, :] = jnp.where(swap, v0, v1).astype(BF16)
        i0 = jnp.broadcast_to(inv[0], (16, 128))
        i1 = jnp.broadcast_to(inv[1], (16, 128))
        invs[0, r, :] = jnp.where(swap, i1, i0)
        invs[1, r, :] = jnp.where(swap, i0, i1)

    loop(0, SEQ // 16, norm_rows)

    def send_norm(j):
        t = lax.rem(slot + j, 8)
        xx = lax.div(t, 2)
        cc = lax.rem(t, 2)
        remote(
            nsend.at[1, t], nrecv.at[1, slot], ns_s.at[1, t], ns_r.at[1, slot], dev(7 - p, xx, mir(c), cc)
        ).start()

        @pl.when(j > 0)
        def _():
            remote(
                nsend.at[0, t], nrecv.at[0, slot], ns_s.at[0, t], ns_r.at[0, slot], dev(p, xx, zh, cc)
            ).start()

    loop(0, 8, send_norm)
    own_norm = pltpu.make_async_copy(nsend.at[0, slot], nrecv.at[0, slot], lsem.at[5])
    own_norm.start()

    eye64 = lax.broadcasted_iota(jnp.int32, (SEQ, SEQ), 0) == lax.broadcasted_iota(
        jnp.int32, (SEQ, SEQ), 1
    )
    row_id = lax.broadcasted_iota(jnp.int32, (SEQ, SEQ), 0)
    col_id = lax.broadcasted_iota(jnp.int32, (SEQ, SEQ), 1)
    for m in range(2):
        start_row = (col_id - pos[m]).astype(F32)
        start_col = jnp.sum(jnp.where(eye64, start_row, 0.0), axis=1, keepdims=True)
        seen = jnp.logical_and(row_id >= col_id, start_row == start_col)
        vis[m] = jnp.where(seen, 1.0, 0.0)
    load_q.wait()
    load_og.wait()
    scale = HD ** (-0.5)

    def attend(i):
        m = lax.div(i, KVH)
        k = lax.rem(i, KVH)
        cols = pl.ds(pl.multiple_of(k * HD, HD), HD)
        heads = [
            pl.ds(pl.multiple_of(k * (GROUP * HD) + g * HD, HD), HD) for g in range(GROUP)
        ]
        kk = keys[m, :, cols]
        vv = values[m, :, cols]
        qs = jnp.concatenate([q[m, :, h] for h in heads], axis=0)
        gs = jnp.concatenate([og[m, :, h] for h in heads], axis=0)
        seen = jnp.concatenate([vis[m]] * GROUP, axis=0) > 0.5
        s = jnp.where(seen, dot(qs, kk, 1, 1) * scale, -1e30)
        w = jnp.exp(s - jnp.max(s, axis=1, keepdims=True))
        probs = w / jnp.sum(w, axis=1, keepdims=True)
        pb = probs.astype(BF16)
        attn = dot(pb, vv, 1, 0).astype(BF16)
        delta = jnp.sum(gs.astype(F32) * attn.astype(F32), axis=1, keepdims=True)
        ds = (probs * (dot(gs, vv, 1, 1) - delta)).astype(BF16)
        qg = (dot(ds, kk, 1, 0) * scale).astype(BF16)
        for g, h in enumerate(heads):
            qg_out[m, :, h] = qg[g * SEQ : (g + 1) * SEQ]
        kvm[m, :, cols] = (dot(ds, qs, 0, 0) * scale).astype(BF16)
        kvm[m, :, pl.ds(pl.multiple_of(KVW + k * HD, HD), HD)] = dot(pb, gs, 0, 0).astype(BF16)

    loop(0, 2 * KVH, attend)

    lane = lax.broadcasted_iota(jnp.int32, (SEQ, 128), 1)

    def split3(v):
        hi = v.astype(BF16).astype(F32)
        mid = (v - hi).astype(BF16).astype(F32)
        low = v - hi - mid
        return jnp.where(lane == 0, hi, jnp.where(lane == 1, mid, low)).astype(BF16)

    kv0 = kvm[0].astype(F32)
    kv1 = kvm[1].astype(F32)
    kvsnd[:, 0:KW] = jnp.where(swap, kv0, kv1).astype(BF16)
    kvsnd[:, KW:KX] = split3(invs[1])
    remote(kvsnd, kvall.at[1, slot], km_s.at[0], km_r.at[0], dev(7 - p, x, mir(c), c)).start()
    kvall[0, slot, :, 0:KW] = jnp.where(swap, kv1, kv0).astype(BF16)
    kvall[0, slot, :, KW:KX] = split3(invs[0])

    def spread_kv(e):
        mine = kvall.at[e, slot]
        for j in (1, 2, 3):
            xx = lax.rem(x + j, 4)
            remote(mine, mine, kx_s.at[e, j], kx_r.at[e, x], dev(p, xx, zh, c)).start()
        remote(mine, mine, kc_s.at[e, x], kc_r.at[e, x], dev(p, x, zh, 1 - c)).start()

    spread_kv(0)
    here(km_s.at[0], km_r.at[0], kvall.at[1, slot]).wait_recv()
    spread_kv(1)
    for e in range(2):
        for j in (1, 3, 2):
            xx = lax.rem(x + j, 4)
            got = kvall.at[e, xx * 2 + c]
            here(kx_s.at[e, j], kx_r.at[e, xx], got).wait_recv()
            remote(got, got, kc_s.at[e, xx], kc_r.at[e, xx], dev(p, x, zh, 1 - c)).start()

    here(w_s.at[0], w_r.at[0], wall.at[zm]).wait_recv()
    first = wall.at[zm, pl.ds(0, HALF)]
    remote(first, first, w_s.at[2], w_r.at[2], dev(p, x, zp, c)).start()
    here(w_s.at[1], w_r.at[1], wall.at[zp]).wait_recv()
    second = wall.at[zp, pl.ds(HALF, HALF)]
    remote(second, second, w_s.at[3], w_r.at[3], dev(p, x, zm, c)).start()

    own_norm.wait()

    def wait_norm(j):
        t = lax.rem(slot + j, 8)
        here(ns_s.at[1, t], ns_r.at[1, t], nrecv.at[1, t]).wait_recv()

        @pl.when(j > 0)
        def _():
            here(ns_s.at[0, t], ns_r.at[0, t], nrecv.at[0, t]).wait_recv()

    loop(0, 8, wait_norm)
    for e in range(2):
        for xx in range(4):
            here(kc_s.at[e, xx], kc_r.at[e, xx], kvall.at[e, xx * 2 + 1 - c]).wait_recv()
    for j, zz in ((1, zm), (2, zf), (3, zp)):
        here(g_s.at[j], g_r.at[j], gall.at[zz]).wait_recv()

    def weight_grad(b, store):
        g = gall[b, 0:1, :].astype(F32)
        for e in range(2):
            n = nrecv[e, :, b].reshape(8 * SEQ, BLK)
            hbuf[e * 8 * SEQ : (e + 1) * 8 * SEQ, :] = (n.astype(F32) * g).astype(BF16)

        def cols(i):
            cc = pl.ds(pl.multiple_of(i * BLK, BLK), BLK)
            kvc = kvall[:, :, :, cc].reshape(16 * SEQ, BLK)
            store(cc, dot(hbuf[...], kvc, 0, 0))

        loop(0, KW // BLK, cols)

    def to_far(cc, v):
        rsf_s[:, cc] = v.astype(BF16)

    weight_grad(zf, to_far)
    remote(rsf_s.at[pl.ds(0, HALF)], rsf_r.at[0], rs_s.at[0], rs_r.at[0], dev(p, x, zp, c)).start()
    remote(rsf_s.at[pl.ds(HALF, HALF)], rsf_r.at[1], rs_s.at[1], rs_r.at[1], dev(p, x, zm, c)).start()
    for i, b in enumerate((zp, zm, zh)):

        def to_part(cc, v, i=i):
            part[i, :, cc] = v

        weight_grad(b, to_part)

    here(w_s.at[2], w_r.at[2], wall.at[zf, pl.ds(0, HALF)]).wait_recv()
    here(w_s.at[3], w_r.at[3], wall.at[zf, pl.ds(HALF, HALF)]).wait_recv()
    cacc[...] = jnp.zeros_like(cacc)

    def hidden_grad(b):
        g = gall[b, 0:1, :].astype(F32)
        total = jnp.zeros((8, BLK), F32)
        for e in range(2):
            hg = dot(kvall[e, :, :, 0:KW].reshape(8 * SEQ, KW), wall[b], 1, 1)
            n = nrecv[e, :, b].reshape(8 * SEQ, BLK).astype(F32)
            total = total + jnp.sum((hg * n).reshape(SEQ, 8, BLK), axis=0)
            ng = (hg * g).astype(BF16)
            ngb[e, :, b] = ng.reshape(8, SEQ, BLK)
            t = ng.astype(F32) * n
            cacc[e] = cacc[e] + t[:, 0:128] + t[:, 128:256]
        gpart[b] = total

    loop(0, 4, hidden_grad)
    eye = lax.broadcasted_iota(jnp.int32, (128, 128), 0) == lax.broadcasted_iota(
        jnp.int32, (128, 128), 1
    )
    for e in range(2):
        for i in range(4):
            col = jnp.sum(cacc[e, i * 128 : (i + 1) * 128, :], axis=1, keepdims=True)
            c_s[e * 4 + i : e * 4 + i + 1, :] = jnp.sum(
                jnp.where(eye, col, 0.0), axis=0, keepdims=True
            )
    c_r[slot] = c_s[...]

    def send_c(j):
        t = lax.rem(slot + j, 8)
        remote(
            c_s, c_r.at[slot], c_ss.at[t], c_rs.at[slot], dev(p, lax.div(t, 2), zh, lax.rem(t, 2))
        ).start()

    loop(1, 8, send_c)
    for j, zz in ((1, zp), (2, zf), (3, zm)):
        remote(gpart.at[zz], gg_r.at[j], gg_ss.at[j], gg_rs.at[j], dev(p, x, zz, c)).start()

    here(rs_s.at[0], rs_r.at[0], rsf_r.at[0]).wait_recv()
    rsn_s[0, 0:HALF, :] = (part[0, 0:HALF, :] + rsf_r[0].astype(F32)).astype(BF16)
    rsn_s[0, HALF:BLK, :] = part[0, HALF:BLK, :].astype(BF16)
    remote(rsn_s.at[0], rsn_r.at[0], rs_s.at[2], rs_r.at[2], dev(p, x, zp, c)).start()
    here(rs_s.at[1], rs_r.at[1], rsf_r.at[1]).wait_recv()
    rsn_s[1, 0:HALF, :] = part[1, 0:HALF, :].astype(BF16)
    rsn_s[1, HALF:BLK, :] = (part[1, HALF:BLK, :] + rsf_r[1].astype(F32)).astype(BF16)
    remote(rsn_s.at[1], rsn_r.at[1], rs_s.at[3], rs_r.at[3], dev(p, x, zm, c)).start()

    def wait_c(j):
        t = lax.rem(slot + j, 8)
        here(c_ss.at[t], c_rs.at[t], c_r.at[t]).wait_recv()

    loop(1, 8, wait_c)
    mean = jnp.sum(c_r[...], axis=0) * (1.0 / D)
    for e in range(2):
        for i in range(4):
            row = mean[e * 4 + i : e * 4 + i + 1, :]
            col = jnp.sum(jnp.where(eye, row, 0.0), axis=1, keepdims=True)
            cbuf[e, 2 * i : 2 * i + 2] = jnp.broadcast_to(col, (128, 128)).reshape(2, SEQ, 128)

    @pl.when(jnp.logical_not(back_down))
    def _():
        brecv[0] = jnp.zeros_like(brecv[0])

    @pl.when(jnp.logical_not(back_up))
    def _():
        brecv[1] = jnp.zeros_like(brecv[1])

    def finish(j):
        t = lax.rem(slot + j, 8)
        xx = lax.div(t, 2)
        cc = lax.rem(t, 2)
        for e in range(2):
            mc = cbuf[e, t][:, 0:1]
            parts3 = kvall[e, t, :, KW:KX].astype(F32)
            inv = jnp.sum(jnp.where(lane < 3, parts3, 0.0), axis=1, keepdims=True)
            for b in range(4):
                n = nrecv[e, t, b].astype(F32)
                bsend[e, t, b] = (inv * (ngb[e, t, b].astype(F32) - n * mc)).astype(BF16)
        is_self = jnp.logical_and(self_up, j == 0)

        @pl.when(back_up)
        def _():
            remote(
                bsend.at[0, t], brecv.at[0, slot], b_s.at[0, t], b_r.at[0, slot], dev(p - 1, xx, zh, cc)
            ).start()

        @pl.when(jnp.logical_and(back_up, jnp.logical_not(is_self)))
        def _():
            remote(
                bsend.at[1, t],
                brecv.at[1, slot],
                b_s.at[1, t],
                b_r.at[1, slot],
                dev(8 - p, xx, mir(cc), cc),
            ).start()

        @pl.when(is_self)
        def _():
            pltpu.make_async_copy(bsend.at[1, t], brecv.at[1, slot], b_r.at[1, slot]).start()

    loop(0, 8, finish)

    here(rs_s.at[2], rs_r.at[2], rsn_r.at[0]).wait_recv()
    here(rs_s.at[3], rs_r.at[3], rsn_r.at[1]).wait_recv()
    wg = part[2] + rsn_r[0].astype(F32) + rsn_r[1].astype(F32)
    wk_out[...] = wg[:, 0:KVW]
    wv_out[...] = wg[:, KVW:KW]
    gg = gpart[zh]
    for j in (1, 2, 3):
        here(gg_ss.at[j], gg_rs.at[j], gg_r.at[j]).wait_recv()
        gg = gg + gg_r[j]
    gg_out[...] = jnp.sum(gg, axis=0, keepdims=True)

    def wait_back(t):
        @pl.when(back_down)
        def _():
            here(b_s.at[0, t], b_r.at[0, t], brecv.at[0, t]).wait_recv()

        @pl.when(back_up)
        def _():
            here(b_s.at[1, t], b_r.at[1, t], brecv.at[1, t]).wait_recv()

    loop(0, 8, wait_back)
    for j in range(32):
        t = (j // 8) * 2 + j % 2
        b = (j // 2) % 4
        down = brecv[0, t, b].astype(F32)
        up = brecv[1, t, b].astype(F32)
        passed_out[0, :, j * BLK : (j + 1) * BLK] = jnp.where(swap, up, down).astype(BF16)
        passed_out[1, :, j * BLK : (j + 1) * BLK] = jnp.where(swap, down, up).astype(BF16)

    def drain(t):
        here(ns_s.at[1, t], ns_r.at[1, t], nsend.at[1, t]).wait_send()

        @pl.when(t != slot)
        def _():
            here(ns_s.at[0, t], ns_r.at[0, t], nsend.at[0, t]).wait_send()
            here(c_ss.at[t], c_rs.at[t], c_s).wait_send()

        @pl.when(back_up)
        def _():
            here(b_s.at[0, t], b_r.at[0, t], bsend.at[0, t]).wait_send()

        @pl.when(jnp.logical_and(back_up, jnp.logical_not(jnp.logical_and(self_up, t == slot))))
        def _():
            here(b_s.at[1, t], b_r.at[1, t], bsend.at[1, t]).wait_send()

    loop(0, 8, drain)
    here(km_s.at[0], km_r.at[0], kvsnd).wait_send()
    for e in range(2):
        for j in (1, 2, 3):
            here(kx_s.at[e, j], kx_r.at[e, j], kvall.at[e, slot]).wait_send()
        for xx in range(4):
            here(kc_s.at[e, xx], kc_r.at[e, xx], kvall.at[e, xx * 2 + c]).wait_send()
    for j in (1, 2, 3):
        here(g_s.at[j], g_r.at[j], gall.at[zh]).wait_send()
        here(gg_ss.at[j], gg_rs.at[j], gg_r.at[j]).wait_send()
    here(w_s.at[0], w_r.at[0], wall.at[zh]).wait_send()
    here(w_s.at[1], w_r.at[1], wall.at[zh]).wait_send()
    here(w_s.at[2], w_r.at[2], first).wait_send()
    here(w_s.at[3], w_r.at[3], second).wait_send()
    here(rs_s.at[0], rs_r.at[0], rsf_r.at[0]).wait_send()
    here(rs_s.at[1], rs_r.at[1], rsf_r.at[1]).wait_send()
    here(rs_s.at[2], rs_r.at[2], rsn_s.at[0]).wait_send()
    here(rs_s.at[3], rs_r.at[3], rsn_s.at[1]).wait_send()


def on_device(
    queries,
    keys,
    values,
    out_grad,
    block_input,
    positions,
    direction,
    key_weight,
    value_weight,
    gain,
):
    vmem = pl.BlockSpec(memory_space=pltpu.VMEM)
    smem = pl.BlockSpec(memory_space=pltpu.SMEM)
    hbm = pl.BlockSpec(memory_space=pl.ANY)
    dma = pltpu.SemaphoreType.DMA
    scratch = [
        pltpu.VMEM((2, SEQ, QW), BF16),
        pltpu.VMEM((2, SEQ, QW), BF16),
        pltpu.VMEM((2, SEQ, D), BF16),
        pltpu.VMEM((2, 8, 4, SEQ, BLK), BF16),
        pltpu.VMEM((2, 8, 4, SEQ, BLK), BF16),
        pltpu.VMEM((2, SEQ, 128), F32),
        pltpu.VMEM((2, SEQ, SEQ), F32),
        pltpu.VMEM((2, SEQ, KW), BF16),
        pltpu.VMEM((SEQ, KX), BF16),
        pltpu.VMEM((2, 8, SEQ, KX), BF16),
        pltpu.VMEM((4, BLK, KW), BF16),
        pltpu.VMEM((4, 16, BLK), BF16),
        pltpu.VMEM((16 * SEQ, BLK), BF16),
        pltpu.VMEM((3, BLK, KW), F32),
        pltpu.VMEM((BLK, KW), BF16),
        pltpu.VMEM((2, HALF, KW), BF16),
        pltpu.VMEM((2, BLK, KW), BF16),
        pltpu.VMEM((2, BLK, KW), BF16),
        pltpu.VMEM((2, 8, 4, SEQ, BLK), BF16),
        pltpu.VMEM((2, 8 * SEQ, 128), F32),
        pltpu.VMEM((4, 8, BLK), F32),
        pltpu.VMEM((4, 8, BLK), F32),
        pltpu.VMEM((8, 128), F32),
        pltpu.VMEM((8, 8, 128), F32),
        pltpu.VMEM((2, 8, SEQ, 128), F32),
        pltpu.VMEM((2, 8, 4, SEQ, BLK), BF16),
        pltpu.VMEM((2, 8, 4, SEQ, BLK), BF16),
        dma((6,)),
        dma((2, 8)),
        dma((2, 8)),
        dma((4,)),
        dma((4,)),
        dma((1,)),
        dma((1,)),
        dma((2, 4)),
        dma((2, 4)),
        dma((2, 4)),
        dma((2, 4)),
        dma((4,)),
        dma((4,)),
        dma((4,)),
        dma((4,)),
        dma((4,)),
        dma((4,)),
        dma((8,)),
        dma((8,)),
        dma((2, 8)),
        dma((2, 8)),
    ]
    qg, passed, wk, wv, gg = pl.pallas_call(
        kernel,
        name="relay",
        out_shape=(
            jax.ShapeDtypeStruct((2, SEQ, QW), BF16),
            jax.ShapeDtypeStruct((2, SEQ, D), BF16),
            jax.ShapeDtypeStruct((BLK, KVW), F32),
            jax.ShapeDtypeStruct((BLK, KVW), F32),
            jax.ShapeDtypeStruct((1, BLK), F32),
        ),
        in_specs=[smem, vmem, vmem, vmem, vmem, hbm, hbm, hbm, hbm, hbm],
        out_specs=(vmem, vmem, vmem, vmem, vmem),
        scratch_shapes=scratch,
        compiler_params=pltpu.CompilerParams(
            collective_id=0, has_side_effects=True, vmem_limit_bytes=56 * 2**20
        ),
    )(
        direction,
        positions.reshape(2, 1, SEQ),
        keys[:, 0],
        values[:, 0],
        gain,
        queries[:, 0],
        out_grad[:, 0],
        block_input[:, 0],
        key_weight[0],
        value_weight[0],
    )
    return qg[:, None], passed[:, None], wk[None], wv[None], gg


def solution(mesh):
    in_specs = (
        P(None, "pipe", "dp", None),
        P(None, "pipe", "dp", None),
        P(None, "pipe", "dp", None),
        P(None, "pipe", "dp", None),
        P(None, "pipe", "dp", None),
        P(None, "pipe", "dp"),
        P(),
        P("pipe", "dp", None),
        P("pipe", "dp", None),
        P("pipe", "dp"),
    )
    out_specs = (
        P(None, "pipe", "dp", None),
        P(None, "pipe", "dp", None),
        P("pipe", "dp", None),
        P("pipe", "dp", None),
        P("pipe", "dp"),
    )
    return jax.shard_map(
        on_device, mesh=mesh, in_specs=in_specs, out_specs=out_specs, check_vma=False
    )
```

time: 328 us -> 169 us (0.52)
  Pallas kernels: 0 us -> 161 us
  waiting for transfers between devices: 150 us -> 0 us
  local copies, waits for them, and re-layouts: 71.7 us -> 5.97 us
  starting transfers between devices: 43.3 us -> 0 us
  matrix products: 24.8 us -> 0 us
  other arithmetic: 21.4 us -> 0 us
  between operations: 15 us -> 0.66 us
    pallas_call x0 -> x1, Pallas kernels: none -> 161 us  [on_device(): pl.pallas_call(kernel, name='relay', out_shape=(jax.ShapeDtypeStruct((2,...]
    ppermute x14 -> x0, waiting for transfers between devices: 150 us -> none  [the longest x12 131 us: swapped_2(): return lax.ppermute(value, axis, pairs)]
    convert_element_type x8 -> x0, local copies, waits for them, and re-layouts: 47.7 us -> none  [the longest x1 14 us: finish_rows(): column_grad = (hidden_grad * gain_stack[:, None, :]).astype(jnp.bfloat16)]
    ppermute x14 -> x0, starting transfers between devices: 22 us -> none  [the longest x12 13.9 us: swapped_2(): return lax.ppermute(value, axis, pairs)]
    dot_general x7 -> x0, matrix products: 22 us -> none  [the longest x1 9.06 us: on_device(): jnp.einsum('tnc,trc->tnr', piece, weight_stack, preferred_element_type=jn...]
    all_to_all x2 -> x0, starting transfers between devices: 21.2 us -> none  [the longest x1 11.8 us: on_device(): lax.all_to_all(normed, 'dp', split_axis=2, concat_axis=1, tiled=True)]
    unnamed x26 -> x13, local copies, waits for them, and re-layouts: 20.4 us -> 5.97 us
    convert_element_type x4 -> x0, other arithmetic: 4.77 us -> none  [the longest x1 1.89 us: attention_grads(): probs_b = probs.astype(jnp.bfloat16)]
  transfers between devices with their start and end apart: 17 -> 0, of which waited for: 8 -> 0; matrix products, arithmetic and copies ran while one was open for 22% -> 0% of each run, Pallas kernels for 0% -> 0%
where the time goes in v1:
time: 169 us; the launch traced here: 168 us
  Pallas kernels  161 us (95%)
  local copies, waits for them, and re-layouts  5.97 us (4%)
    pallas_call x1, Pallas kernels, on_device(): pl.pallas_call(kernel, name='relay', out_shape=(jax.ShapeDtypeStruct((2,...  161 us
    unnamed x13, local copies, waits for them, and re-layouts  5.97 us

profile of v1, /device:TPU:30, one launch (start us, length us, event | category | flops | bytes accessed | tf_op | source)
XLA Modules:
  0.0 167.5 jit_solution(6819412060207763606)
XLA Ops:
  0.6 160.9 %relay.1 = (bf16[2,64,4096]{2,1,0:T(8,128)(2,1)}, bf16[2,64,8192]{2,1,0:T(8,128)(2,1)}, f32[256,512]{1,0:T(8,128)}, f32[256,512]{1,0:T(8,128)}, f32[1,256]{1,0:T(1,128)}) custom-call(s32[2]{0:T(128)} %flag.1, s32[2,1,64]{2,1,0:T(1,128)} %pos.1, bf16[2,64,512]{2,1,0:T(8,128)(2,1)} %bitcast.24, bf16[2,64,512]{2,1,0:T(8,128)(2,1)} %bitcast.25, ...), custom_call_target="tpu_custom_call" | custom-call | tf_op jit(solution)/shard_map/relay/pallas_call | solution.py:584
  161.6 0.0 copy-start
  161.6 2.4 %copy.22 = bf16[2,1,64,4096]{3,2,1,0:T(8,128)(2,1)} copy(bf16[2,1,64,4096]{3,2,1,0:T(8,128)(2,1)} %bitcast.19) | data formatting | bytes 2097152
  164.0 0.0 copy-done
  164.0 0.0 copy-start.2
  164.0 0.0 copy-start.1
  164.0 1.3 copy.23
  165.3 0.1 copy-done.2
  165.4 0.0 copy-start.3
  165.4 0.8 copy.24
  166.2 0.0 copy-done.1
  166.2 0.8 copy.25
  167.0 0.0 copy-done.3
  167.0 0.6 copy.26
Async XLA Ops:
  161.6 2.4 %copy-start = (bf16[2,64,8192]{2,1,0:T(8,128)(2,1)S(1)}, bf16[2,64,8192]{2,1,0:T(8,128)(2,1)}, u32[]{:S(2)}) copy-start(bf16[2,64,8192]{2,1,0:T(8,128)(2,1)} %get-tuple-element.11) | copy-start | bytes 6291460
  164.0 1.4 copy-start.2
  164.0 2.2 %copy-start.1 = (f32[256,512]{1,0:T(8,128)S(1)}, f32[256,512]{1,0:T(8,128)}, u32[]{:S(2)}) copy-start(f32[256,512]{1,0:T(8,128)} %get-tuple-element.13) | copy-start | bytes 1572868
  165.4 1.6 copy-start.3

commit v2 on v1

--- a/solution.py
+++ b/solution.py
@@ -18,6 +18,7 @@
 KW = 2 * KVW
 KX = KW + 128
 HALF = BLK // 2
+MOST = HALF + HALF // 2
 MESH = pl.DeviceIdType.MESH
 F32 = jnp.float32
 BF16 = jnp.bfloat16
@@ -38,11 +39,12 @@
     inp_hbm,
     kw_hbm,
     vw_hbm,
-    qg_out,
+    qg_hbm,
     passed_out,
     wk_out,
     wv_out,
     gg_out,
+    qg,
     q,
     og,
     inp,
@@ -57,6 +59,7 @@
     gall,
     hbuf,
     part,
+    own,
     rsf_s,
     rsf_r,
     rsn_s,
@@ -70,6 +73,7 @@
     cbuf,
     bsend,
     brecv,
+    relay,
     lsem,
     ns_s,
     ns_r,
@@ -91,6 +95,8 @@
     c_rs,
     b_s,
     b_r,
+    u_s,
+    u_r,
 ):
     p = lax.axis_index("pipe")
     d = lax.axis_index("dp")
@@ -146,8 +152,15 @@
     zlm = lax.div(p + 3, 4) - 1
     zup = lax.rem(zh + 4 + c * (2 * zlm - 1), 4)
 
+    even = lax.rem(p, 2) == 0
+    odd = jnp.logical_not(even)
+    even_up = jnp.logical_and(even, back_up)
     for zz in (zp, zm, zf):
         greet(dev(p, x, zz, c))
+
+    @pl.when(odd)
+    def _():
+        greet(dev(p - 1, x, zh, c))
 
     def greet_all(j):
         t = lax.rem(slot + j, 8)
@@ -164,21 +177,16 @@
         def _():
             greet(dev(p + 1, xx, zh, cc))
 
-        @pl.when(jnp.logical_and(back_up, jnp.logical_not(jnp.logical_and(self_up, j == 0))))
+        @pl.when(even)
+        def _():
+            greet(dev(7 - p, xx, mir(c), cc))
+
+        @pl.when(jnp.logical_and(even_up, jnp.logical_not(jnp.logical_and(self_up, j == 0))))
         def _():
             greet(dev(8 - p, xx, zup, cc))
 
     loop(0, 8, greet_all)
     gall[zh] = jnp.broadcast_to(gain[...], (16, BLK))
-    n_back = jnp.where(back_up, 16, 0) - jnp.where(self_up, 1, 0)
-    pl.semaphore_wait(bar, 18 + n_back)
-
-    for j, zz in ((1, zp), (2, zf), (3, zm)):
-        remote(gall.at[zh], gall.at[zh], g_s.at[j], g_r.at[j], dev(p, x, zz, c)).start()
-    load_kw.wait()
-    load_vw.wait()
-    remote(wall.at[zh], wall.at[zh], w_s.at[0], w_r.at[0], dev(p, x, zp, c)).start()
-    remote(wall.at[zh], wall.at[zh], w_s.at[1], w_r.at[1], dev(p, x, zm, c)).start()
 
     swap = flag[0] == 1
     load_inp.wait()
@@ -205,23 +213,24 @@
 
     loop(0, SEQ // 16, norm_rows)
 
-    def send_norm(j):
-        t = lax.rem(slot + j, 8)
-        xx = lax.div(t, 2)
-        cc = lax.rem(t, 2)
-        remote(
-            nsend.at[1, t], nrecv.at[1, slot], ns_s.at[1, t], ns_r.at[1, slot], dev(7 - p, xx, mir(c), cc)
-        ).start()
-
-        @pl.when(j > 0)
-        def _():
-            remote(
-                nsend.at[0, t], nrecv.at[0, slot], ns_s.at[0, t], ns_r.at[0, slot], dev(p, xx, zh, cc)
-            ).start()
-
-    loop(0, 8, send_norm)
-    own_norm = pltpu.make_async_copy(nsend.at[0, slot], nrecv.at[0, slot], lsem.at[5])
-    own_norm.start()
+    n_back = jnp.where(back_up, 16, 0) - jnp.where(self_up, 1, 0) + jnp.where(even, 1, 0)
+    pl.semaphore_wait(bar, 18 + n_back)
+
+    low = pl.ds(0, HALF)
+    high = pl.ds(HALF, HALF)
+
+    def send_w(zz, part_rows, i, to):
+        ref = wall.at[zz, part_rows]
+        remote(ref, ref, w_s.at[i], w_r.at[i], dev(p, x, to, c)).start()
+
+    load_kw.wait()
+    load_vw.wait()
+    send_w(zh, low, 0, zp)
+    send_w(zh, high, 3, zm)
+    send_w(zh, high, 1, zp)
+    send_w(zh, low, 2, zm)
+    for j, zz in ((1, zp), (2, zf), (3, zm)):
+        remote(gall.at[zh], gall.at[zh], g_s.at[j], g_r.at[j], dev(p, x, zz, c)).start()
 
     eye64 = lax.broadcasted_iota(jnp.int32, (SEQ, SEQ), 0) == lax.broadcasted_iota(
         jnp.int32, (SEQ, SEQ), 1
@@ -256,13 +265,15 @@
         attn = dot(pb, vv, 1, 0).astype(BF16)
         delta = jnp.sum(gs.astype(F32) * attn.astype(F32), axis=1, keepdims=True)
         ds = (probs * (dot(gs, vv, 1, 1) - delta)).astype(BF16)
-        qg = (dot(ds, kk, 1, 0) * scale).astype(BF16)
+        qgs = (dot(ds, kk, 1, 0) * scale).astype(BF16)
         for g, h in enumerate(heads):
-            qg_out[m, :, h] = qg[g * SEQ : (g + 1) * SEQ]
+            qg[m, :, h] = qgs[g * SEQ : (g + 1) * SEQ]
         kvm[m, :, cols] = (dot(ds, qs, 0, 0) * scale).astype(BF16)
         kvm[m, :, pl.ds(pl.multiple_of(KVW + k * HD, HD), HD)] = dot(pb, gs, 0, 0).astype(BF16)
 
     loop(0, 2 * KVH, attend)
+    store_qg = pltpu.make_async_copy(qg, qg_hbm, lsem.at[6])
+    store_qg.start()
 
     lane = lax.broadcasted_iota(jnp.int32, (SEQ, 128), 1)
 
@@ -288,8 +299,35 @@
         remote(mine, mine, kc_s.at[e, x], kc_r.at[e, x], dev(p, x, zh, 1 - c)).start()
 
     spread_kv(0)
+
+    def send_norm(j):
+        t = lax.rem(slot + j, 8)
+        xx = lax.div(t, 2)
+        cc = lax.rem(t, 2)
+        remote(
+            nsend.at[1, t], nrecv.at[1, slot], ns_s.at[1, t], ns_r.at[1, slot], dev(7 - p, xx, mir(c), cc)
+        ).start()
+
+        @pl.when(j > 0)
+        def _():
+            remote(
+                nsend.at[0, t], nrecv.at[0, slot], ns_s.at[0, t], ns_r.at[0, slot], dev(p, xx, zh, cc)
+            ).start()
+
+    loop(0, 8, send_norm)
+    own_norm = pltpu.make_async_copy(nsend.at[0, slot], nrecv.at[0, slot], lsem.at[5])
+    own_norm.start()
+
     here(km_s.at[0], km_r.at[0], kvall.at[1, slot]).wait_recv()
     spread_kv(1)
+    def got_w(zz, part_rows, i):
+        here(w_s.at[i], w_r.at[i], wall.at[zz, part_rows]).wait_recv()
+
+    got_w(zm, low, 0)
+    send_w(zm, low, 4, zp)
+    got_w(zp, high, 3)
+    send_w(zp, high, 5, zm)
+
     for e in range(2):
         for j in (1, 3, 2):
             xx = lax.rem(x + j, 4)
@@ -297,13 +335,6 @@
             here(kx_s.at[e, j], kx_r.at[e, xx], got).wait_recv()
             remote(got, got, kc_s.at[e, xx], kc_r.at[e, xx], dev(p, x, zh, 1 - c)).start()
 
-    here(w_s.at[0], w_r.at[0], wall.at[zm]).wait_recv()
-    first = wall.at[zm, pl.ds(0, HALF)]
-    remote(first, first, w_s.at[2], w_r.at[2], dev(p, x, zp, c)).start()
-    here(w_s.at[1], w_r.at[1], wall.at[zp]).wait_recv()
-    second = wall.at[zp, pl.ds(HALF, HALF)]
-    remote(second, second, w_s.at[3], w_r.at[3], dev(p, x, zm, c)).start()
-
     own_norm.wait()
 
     def wait_norm(j):
@@ -334,21 +365,39 @@
 
         loop(0, KW // BLK, cols)
 
+    def send_rs(src, dst, i, to):
+        remote(src, dst, rs_s.at[i], rs_r.at[i], dev(p, x, to, c)).start()
+
     def to_far(cc, v):
         rsf_s[:, cc] = v.astype(BF16)
 
+    def to_next(cc, v):
+        part[0, 0:MOST, cc] = v[0:MOST]
+        rsn_s[0, MOST:BLK, cc] = v[MOST:BLK].astype(BF16)
+
+    def to_prev(cc, v):
+        part[1, 0:HALF, cc] = v[HALF:BLK]
+        rsn_s[1, 0:HALF, cc] = v[0:HALF].astype(BF16)
+
+    def to_own(cc, v):
+        own[:, cc] = v
+
+    third = pl.ds(HALF, HALF // 2)
+    fourth = pl.ds(HALF + HALF // 2, HALF // 2)
+    upward = lax.rem(p, 4) == 0
     weight_grad(zf, to_far)
-    remote(rsf_s.at[pl.ds(0, HALF)], rsf_r.at[0], rs_s.at[0], rs_r.at[0], dev(p, x, zp, c)).start()
-    remote(rsf_s.at[pl.ds(HALF, HALF)], rsf_r.at[1], rs_s.at[1], rs_r.at[1], dev(p, x, zm, c)).start()
-    for i, b in enumerate((zp, zm, zh)):
-
-        def to_part(cc, v, i=i):
-            part[i, :, cc] = v
-
-        weight_grad(b, to_part)
-
-    here(w_s.at[2], w_r.at[2], wall.at[zf, pl.ds(0, HALF)]).wait_recv()
-    here(w_s.at[3], w_r.at[3], wall.at[zf, pl.ds(HALF, HALF)]).wait_recv()
+    send_rs(rsf_s.at[low], rsf_r.at[low], 0, zp)
+    send_rs(rsf_s.at[third], rsf_r.at[third], 1, jnp.where(upward, zp, zm))
+    send_rs(rsf_s.at[fourth], rsf_r.at[fourth], 2, zm)
+    weight_grad(zp, to_next)
+    send_rs(rsn_s.at[0, fourth], rsn_r.at[0, fourth], 3, zp)
+    weight_grad(zm, to_prev)
+    send_rs(rsn_s.at[1, low], rsn_r.at[1, low], 4, zm)
+
+    got_w(zm, high, 1)
+    got_w(zp, low, 2)
+    got_w(zf, low, 4)
+    got_w(zf, high, 5)
     cacc[...] = jnp.zeros_like(cacc)
 
     def hidden_grad(b):
@@ -386,15 +435,6 @@
     for j, zz in ((1, zp), (2, zf), (3, zm)):
         remote(gpart.at[zz], gg_r.at[j], gg_ss.at[j], gg_rs.at[j], dev(p, x, zz, c)).start()
 
-    here(rs_s.at[0], rs_r.at[0], rsf_r.at[0]).wait_recv()
-    rsn_s[0, 0:HALF, :] = (part[0, 0:HALF, :] + rsf_r[0].astype(F32)).astype(BF16)
-    rsn_s[0, HALF:BLK, :] = part[0, HALF:BLK, :].astype(BF16)
-    remote(rsn_s.at[0], rsn_r.at[0], rs_s.at[2], rs_r.at[2], dev(p, x, zp, c)).start()
-    here(rs_s.at[1], rs_r.at[1], rsf_r.at[1]).wait_recv()
-    rsn_s[1, 0:HALF, :] = part[1, 0:HALF, :].astype(BF16)
-    rsn_s[1, HALF:BLK, :] = (part[1, HALF:BLK, :] + rsf_r[1].astype(F32)).astype(BF16)
-    remote(rsn_s.at[1], rsn_r.at[1], rs_s.at[3], rs_r.at[3], dev(p, x, zm, c)).start()
-
     def wait_c(j):
         t = lax.rem(slot + j, 8)
         here(c_ss.at[t], c_rs.at[t], c_r.at[t]).wait_recv()
@@ -434,7 +474,13 @@
                 bsend.at[0, t], brecv.at[0, slot], b_s.at[0, t], b_r.at[0, slot], dev(p - 1, xx, zh, cc)
             ).start()
 
-        @pl.when(jnp.logical_and(back_up, jnp.logical_not(is_self)))
+        @pl.when(odd)
+        def _():
+            remote(
+                bsend.at[1, t], relay.at[slot], b_s.at[1, t], u_r.at[slot], dev(7 - p, xx, mir(cc), cc)
+            ).start()
+
+        @pl.when(jnp.logical_and(even_up, jnp.logical_not(is_self)))
         def _():
             remote(
                 bsend.at[1, t],
@@ -450,9 +496,33 @@
 
     loop(0, 8, finish)
 
-    here(rs_s.at[2], rs_r.at[2], rsn_r.at[0]).wait_recv()
-    here(rs_s.at[3], rs_r.at[3], rsn_r.at[1]).wait_recv()
-    wg = part[2] + rsn_r[0].astype(F32) + rsn_r[1].astype(F32)
+    here(rs_s.at[0], rs_r.at[0], rsf_r.at[low]).wait_recv()
+    rsn_s[0, 0:HALF, :] = (part[0, 0:HALF, :] + rsf_r[0:HALF, :].astype(F32)).astype(BF16)
+    send_rs(rsn_s.at[0, low], rsn_r.at[0, low], 5, zp)
+    here(rs_s.at[1], rs_r.at[1], rsf_r.at[third]).wait_recv()
+    more = rsf_r[HALF:MOST, :].astype(F32)
+    rsn_s[0, HALF:MOST, :] = (part[0, HALF:MOST, :] + jnp.where(upward, more, 0.0)).astype(BF16)
+    send_rs(rsn_s.at[0, third], rsn_r.at[0, third], 7, zp)
+    rsn_s[1, HALF:MOST, :] = (part[1, 0 : MOST - HALF, :] + jnp.where(upward, 0.0, more)).astype(BF16)
+    send_rs(rsn_s.at[1, third], rsn_r.at[1, third], 8, zm)
+    here(rs_s.at[2], rs_r.at[2], rsf_r.at[fourth]).wait_recv()
+    rsn_s[1, MOST:BLK, :] = (part[1, MOST - HALF : HALF, :] + rsf_r[MOST:BLK, :].astype(F32)).astype(BF16)
+    send_rs(rsn_s.at[1, fourth], rsn_r.at[1, fourth], 6, zm)
+
+    weight_grad(zh, to_own)
+
+    def pass_on(t):
+        here(u_s.at[t], u_r.at[t], relay.at[t]).wait_recv()
+        remote(relay.at[t], brecv.at[1, t], u_s.at[t], b_r.at[1, t], dev(p + 1, x, zh, c)).start()
+
+    @pl.when(even)
+    def _():
+        loop(0, 8, pass_on)
+
+    near = ((3, 0, fourth), (4, 1, low), (5, 0, low), (6, 1, fourth), (7, 0, third), (8, 1, third))
+    for i, side, piece in near:
+        here(rs_s.at[i], rs_r.at[i], rsn_r.at[side, piece]).wait_recv()
+    wg = own[...] + rsn_r[0].astype(F32) + rsn_r[1].astype(F32)
     wk_out[...] = wg[:, 0:KVW]
     wv_out[...] = wg[:, KVW:KW]
     gg = gpart[zh]
@@ -486,6 +556,10 @@
         def _():
             here(ns_s.at[0, t], ns_r.at[0, t], nsend.at[0, t]).wait_send()
             here(c_ss.at[t], c_rs.at[t], c_s).wait_send()
+
+        @pl.when(even)
+        def _():
+            here(u_s.at[t], u_r.at[t], relay.at[t]).wait_send()
 
         @pl.when(back_up)
         def _():
@@ -505,14 +579,13 @@
     for j in (1, 2, 3):
         here(g_s.at[j], g_r.at[j], gall.at[zh]).wait_send()
         here(gg_ss.at[j], gg_rs.at[j], gg_r.at[j]).wait_send()
-    here(w_s.at[0], w_r.at[0], wall.at[zh]).wait_send()
-    here(w_s.at[1], w_r.at[1], wall.at[zh]).wait_send()
-    here(w_s.at[2], w_r.at[2], first).wait_send()
-    here(w_s.at[3], w_r.at[3], second).wait_send()
-    here(rs_s.at[0], rs_r.at[0], rsf_r.at[0]).wait_send()
-    here(rs_s.at[1], rs_r.at[1], rsf_r.at[1]).wait_send()
-    here(rs_s.at[2], rs_r.at[2], rsn_s.at[0]).wait_send()
-    here(rs_s.at[3], rs_r.at[3], rsn_s.at[1]).wait_send()
+    for i in range(6):
+        here(w_s.at[i], w_r.at[i], wall.at[zh, low]).wait_send()
+    for i, piece in ((0, low), (1, third), (2, fourth)):
+        here(rs_s.at[i], rs_r.at[i], rsf_s.at[piece]).wait_send()
+    for i, side, piece in near:
+        here(rs_s.at[i], rs_r.at[i], rsn_s.at[side, piece]).wait_send()
+    store_qg.wait()
 
 
 def on_device(
@@ -534,6 +607,7 @@
     scratch = [
         pltpu.VMEM((2, SEQ, QW), BF16),
         pltpu.VMEM((2, SEQ, QW), BF16),
+        pltpu.VMEM((2, SEQ, QW), BF16),
         pltpu.VMEM((2, SEQ, D), BF16),
         pltpu.VMEM((2, 8, 4, SEQ, BLK), BF16),
         pltpu.VMEM((2, 8, 4, SEQ, BLK), BF16),
@@ -545,9 +619,10 @@
         pltpu.VMEM((4, BLK, KW), BF16),
         pltpu.VMEM((4, 16, BLK), BF16),
         pltpu.VMEM((16 * SEQ, BLK), BF16),
-        pltpu.VMEM((3, BLK, KW), F32),
+        pltpu.VMEM((2, MOST, KW), F32),
+        pltpu.VMEM((BLK, KW), F32),
         pltpu.VMEM((BLK, KW), BF16),
-        pltpu.VMEM((2, HALF, KW), BF16),
+        pltpu.VMEM((BLK, KW), BF16),
         pltpu.VMEM((2, BLK, KW), BF16),
         pltpu.VMEM((2, BLK, KW), BF16),
         pltpu.VMEM((2, 8, 4, SEQ, BLK), BF16),
@@ -559,7 +634,8 @@
         pltpu.VMEM((2, 8, SEQ, 128), F32),
         pltpu.VMEM((2, 8, 4, SEQ, BLK), BF16),
         pltpu.VMEM((2, 8, 4, SEQ, BLK), BF16),
-        dma((6,)),
+        pltpu.VMEM((8, 4, SEQ, BLK), BF16),
+        dma((7,)),
         dma((2, 8)),
         dma((2, 8)),
         dma((4,)),
@@ -570,16 +646,18 @@
         dma((2, 4)),
         dma((2, 4)),
         dma((2, 4)),
-        dma((4,)),
-        dma((4,)),
-        dma((4,)),
-        dma((4,)),
+        dma((6,)),
+        dma((6,)),
+        dma((9,)),
+        dma((9,)),
         dma((4,)),
         dma((4,)),
         dma((8,)),
         dma((8,)),
         dma((2, 8)),
         dma((2, 8)),
+        dma((8,)),
+        dma((8,)),
     ]
     qg, passed, wk, wv, gg = pl.pallas_call(
         kernel,
@@ -592,7 +670,7 @@
             jax.ShapeDtypeStruct((1, BLK), F32),
         ),
         in_specs=[smem, vmem, vmem, vmem, vmem, hbm, hbm, hbm, hbm, hbm],
-        out_specs=(vmem, vmem, vmem, vmem, vmem),
+        out_specs=(hbm, vmem, vmem, vmem, vmem),
         scratch_shapes=scratch,
         compiler_params=pltpu.CompilerParams(
             collective_id=0, has_side_effects=True, vmem_limit_bytes=56 * 2**20

time: 169 us -> 140 us (0.83)
  Pallas kernels: 161 us -> 133 us
    pallas_call x1, Pallas kernels: 161 us -> 133 us  [on_device(): pl.pallas_call(kernel, name='relay', out_shape=(jax.ShapeDtypeStruct((2,...]
where the time goes in v2:
time: 140 us
  Pallas kernels  133 us (95%)
  local copies, waits for them, and re-layouts  5.97 us (4%)
    pallas_call x1, Pallas kernels, on_device(): pl.pallas_call(kernel, name='relay', out_shape=(jax.ShapeDtypeStruct((2,...  133 us
    unnamed x13, local copies, waits for them, and re-layouts  5.97 us

profile of v2, /device:TPU:30, one launch (start us, length us, event | category | flops | bytes accessed | tf_op | source)
XLA Modules:
  0.0 139.6 jit_solution(11468532061508015084)
XLA Ops:
  0.6 133.0 %relay.1 = (bf16[2,64,4096]{2,1,0:T(8,128)(2,1)}, bf16[2,64,8192]{2,1,0:T(8,128)(2,1)}, f32[256,512]{1,0:T(8,128)}, f32[256,512]{1,0:T(8,128)}, f32[1,256]{1,0:T(1,128)}) custom-call(s32[2]{0:T(128)} %flag.1, s32[2,1,64]{2,1,0:T(1,128)} %pos.1, bf16[2,64,512]{2,1,0:T(8,128)(2,1)} %bitcast.24, bf16[2,64,512]{2,1,0:T(8,128)(2,1)} %bitcast.25, ...), custom_call_target="tpu_custom_call" | custom-call | tf_op jit(solution)/shard_map/relay/pallas_call | solution.py:662
  133.6 0.0 copy-start
  133.6 2.4 %copy.22 = bf16[2,1,64,4096]{3,2,1,0:T(8,128)(2,1)} copy(bf16[2,1,64,4096]{3,2,1,0:T(8,128)(2,1)} %bitcast.19) | data formatting | bytes 2097152
  136.1 0.0 copy-done
  136.1 0.0 copy-start.2
  136.1 0.0 copy-start.1
  136.1 1.3 copy.23
  137.4 0.1 copy-done.2
  137.4 0.0 copy-start.3
  137.4 0.8 copy.24
  138.2 0.0 copy-done.1
  138.2 0.8 copy.25
  139.0 0.0 copy-done.3
  139.0 0.6 copy.26
Async XLA Ops:
  133.6 2.4 %copy-start = (bf16[2,64,8192]{2,1,0:T(8,128)(2,1)S(1)}, bf16[2,64,8192]{2,1,0:T(8,128)(2,1)}, u32[]{:S(2)}) copy-start(bf16[2,64,8192]{2,1,0:T(8,128)(2,1)} %get-tuple-element.11) | copy-start | bytes 6291460
  136.1 1.4 copy-start.2
  136.1 2.2 %copy-start.1 = (f32[256,512]{1,0:T(8,128)S(1)}, f32[256,512]{1,0:T(8,128)}, u32[]{:S(2)}) copy-start(f32[256,512]{1,0:T(8,128)} %get-tuple-element.13) | copy-start | bytes 1572868
  137.4 1.6 %copy-start.3 = (f32[1,256]{1,0:T(1,128)S(1)}, f32[1,256]{1,0:T(1,128)}, u32[]{:S(2)}) copy-start(f32[1,256]{1,0:T(1,128)} %get-tuple-element.29) | copy-start | bytes 3076

commit v3 on v2

--- a/solution.py
+++ b/solution.py
@@ -67,6 +67,7 @@
     ngb,
     cacc,
     gpart,
+    gsum,
     gg_r,
     c_s,
     c_r,
@@ -232,6 +233,15 @@
     for j, zz in ((1, zp), (2, zf), (3, zm)):
         remote(gall.at[zh], gall.at[zh], g_s.at[j], g_r.at[j], dev(p, x, zz, c)).start()
 
+    def send_down(j):
+        t = lax.rem(slot + j, 8)
+        to = dev(p, lax.div(t, 2), zh, lax.rem(t, 2))
+        remote(nsend.at[0, t], nrecv.at[0, slot], ns_s.at[0, t], ns_r.at[0, slot], to).start()
+
+    loop(1, 8, send_down)
+    own_norm = pltpu.make_async_copy(nsend.at[0, slot], nrecv.at[0, slot], lsem.at[5])
+    own_norm.start()
+
     eye64 = lax.broadcasted_iota(jnp.int32, (SEQ, SEQ), 0) == lax.broadcasted_iota(
         jnp.int32, (SEQ, SEQ), 1
     )
@@ -300,23 +310,12 @@
 
     spread_kv(0)
 
-    def send_norm(j):
+    def send_up(j):
         t = lax.rem(slot + j, 8)
-        xx = lax.div(t, 2)
-        cc = lax.rem(t, 2)
-        remote(
-            nsend.at[1, t], nrecv.at[1, slot], ns_s.at[1, t], ns_r.at[1, slot], dev(7 - p, xx, mir(c), cc)
-        ).start()
-
-        @pl.when(j > 0)
-        def _():
-            remote(
-                nsend.at[0, t], nrecv.at[0, slot], ns_s.at[0, t], ns_r.at[0, slot], dev(p, xx, zh, cc)
-            ).start()
-
-    loop(0, 8, send_norm)
-    own_norm = pltpu.make_async_copy(nsend.at[0, slot], nrecv.at[0, slot], lsem.at[5])
-    own_norm.start()
+        to = dev(7 - p, lax.div(t, 2), mir(c), lax.rem(t, 2))
+        remote(nsend.at[1, t], nrecv.at[1, slot], ns_s.at[1, t], ns_r.at[1, slot], to).start()
+
+    loop(0, 8, send_up)
 
     here(km_s.at[0], km_r.at[0], kvall.at[1, slot]).wait_recv()
     spread_kv(1)
@@ -399,53 +398,39 @@
     got_w(zf, low, 4)
     got_w(zf, high, 5)
     cacc[...] = jnp.zeros_like(cacc)
-
-    def hidden_grad(b):
-        g = gall[b, 0:1, :].astype(F32)
-        total = jnp.zeros((8, BLK), F32)
-        for e in range(2):
+    eye = lax.broadcasted_iota(jnp.int32, (128, 128), 0) == lax.broadcasted_iota(
+        jnp.int32, (128, 128), 1
+    )
+
+    def hidden_grad(e):
+        def block(b):
+            g = gall[b, 0:1, :].astype(F32)
             hg = dot(kvall[e, :, :, 0:KW].reshape(8 * SEQ, KW), wall[b], 1, 1)
             n = nrecv[e, :, b].reshape(8 * SEQ, BLK).astype(F32)
-            total = total + jnp.sum((hg * n).reshape(SEQ, 8, BLK), axis=0)
+            gpart[e, b] = jnp.sum((hg * n).reshape(SEQ, 8, BLK), axis=0)
             ng = (hg * g).astype(BF16)
             ngb[e, :, b] = ng.reshape(8, SEQ, BLK)
             t = ng.astype(F32) * n
             cacc[e] = cacc[e] + t[:, 0:128] + t[:, 128:256]
-        gpart[b] = total
-
-    loop(0, 4, hidden_grad)
-    eye = lax.broadcasted_iota(jnp.int32, (128, 128), 0) == lax.broadcasted_iota(
-        jnp.int32, (128, 128), 1
-    )
-    for e in range(2):
+
+        loop(0, 4, block)
         for i in range(4):
             col = jnp.sum(cacc[e, i * 128 : (i + 1) * 128, :], axis=1, keepdims=True)
-            c_s[e * 4 + i : e * 4 + i + 1, :] = jnp.sum(
-                jnp.where(eye, col, 0.0), axis=0, keepdims=True
-            )
-    c_r[slot] = c_s[...]
-
-    def send_c(j):
-        t = lax.rem(slot + j, 8)
-        remote(
-            c_s, c_r.at[slot], c_ss.at[t], c_rs.at[slot], dev(p, lax.div(t, 2), zh, lax.rem(t, 2))
-        ).start()
-
-    loop(1, 8, send_c)
+            c_s[e, i : i + 1, :] = jnp.sum(jnp.where(eye, col, 0.0), axis=0, keepdims=True)
+        c_r[e, slot] = c_s[e]
+
+        def send_c(j):
+            t = lax.rem(slot + j, 8)
+            to = dev(p, lax.div(t, 2), zh, lax.rem(t, 2))
+            remote(c_s.at[e], c_r.at[e, slot], c_ss.at[e, t], c_rs.at[e, slot], to).start()
+
+        loop(1, 8, send_c)
+
+    hidden_grad(1)
+    hidden_grad(0)
+    gsum[...] = gpart[0] + gpart[1]
     for j, zz in ((1, zp), (2, zf), (3, zm)):
-        remote(gpart.at[zz], gg_r.at[j], gg_ss.at[j], gg_rs.at[j], dev(p, x, zz, c)).start()
-
-    def wait_c(j):
-        t = lax.rem(slot + j, 8)
-        here(c_ss.at[t], c_rs.at[t], c_r.at[t]).wait_recv()
-
-    loop(1, 8, wait_c)
-    mean = jnp.sum(c_r[...], axis=0) * (1.0 / D)
-    for e in range(2):
-        for i in range(4):
-            row = mean[e * 4 + i : e * 4 + i + 1, :]
-            col = jnp.sum(jnp.where(eye, row, 0.0), axis=1, keepdims=True)
-            cbuf[e, 2 * i : 2 * i + 2] = jnp.broadcast_to(col, (128, 128)).reshape(2, SEQ, 128)
+        remote(gsum.at[zz], gg_r.at[j], gg_ss.at[j], gg_rs.at[j], dev(p, x, zz, c)).start()
 
     @pl.when(jnp.logical_not(back_down))
     def _():
@@ -455,46 +440,64 @@
     def _():
         brecv[1] = jnp.zeros_like(brecv[1])
 
-    def finish(j):
-        t = lax.rem(slot + j, 8)
-        xx = lax.div(t, 2)
-        cc = lax.rem(t, 2)
-        for e in range(2):
+    def branch(e):
+        def wait_c(j):
+            t = lax.rem(slot + j, 8)
+            here(c_ss.at[e, t], c_rs.at[e, t], c_r.at[e, t]).wait_recv()
+
+        loop(1, 8, wait_c)
+        mean = jnp.sum(c_r[e], axis=0) * (1.0 / D)
+        for i in range(4):
+            col = jnp.sum(jnp.where(eye, mean[i : i + 1, :], 0.0), axis=1, keepdims=True)
+            cbuf[e, 2 * i : 2 * i + 2] = jnp.broadcast_to(col, (128, 128)).reshape(2, SEQ, 128)
+
+        def chunk(t):
             mc = cbuf[e, t][:, 0:1]
             parts3 = kvall[e, t, :, KW:KX].astype(F32)
             inv = jnp.sum(jnp.where(lane < 3, parts3, 0.0), axis=1, keepdims=True)
             for b in range(4):
                 n = nrecv[e, t, b].astype(F32)
                 bsend[e, t, b] = (inv * (ngb[e, t, b].astype(F32) - n * mc)).astype(BF16)
+
+        loop(0, 8, chunk)
+
+    branch(1)
+    branch(0)
+
+    def pass_on(j):
+        t = lax.rem(slot - j + 8, 8)
+
+        @pl.when(even)
+        def _():
+            here(u_s.at[t], u_r.at[t], relay.at[t]).wait_recv()
+            remote(relay.at[t], brecv.at[1, t], u_s.at[t], b_r.at[1, t], dev(p + 1, x, zh, c)).start()
+
+    def send_back(j):
+        t = lax.rem(slot + j, 8)
+        xx = lax.div(t, 2)
+        cc = lax.rem(t, 2)
         is_self = jnp.logical_and(self_up, j == 0)
 
+        @pl.when(odd)
+        def _():
+            to = dev(7 - p, xx, mir(cc), cc)
+            remote(bsend.at[1, t], relay.at[slot], b_s.at[1, t], u_r.at[slot], to).start()
+
+        @pl.when(jnp.logical_and(even_up, jnp.logical_not(is_self)))
+        def _():
+            to = dev(8 - p, xx, mir(cc), cc)
+            remote(bsend.at[1, t], brecv.at[1, slot], b_s.at[1, t], b_r.at[1, slot], to).start()
+
+        @pl.when(is_self)
+        def _():
+            pltpu.make_async_copy(bsend.at[1, t], brecv.at[1, slot], b_r.at[1, slot]).start()
+
         @pl.when(back_up)
         def _():
-            remote(
-                bsend.at[0, t], brecv.at[0, slot], b_s.at[0, t], b_r.at[0, slot], dev(p - 1, xx, zh, cc)
-            ).start()
-
-        @pl.when(odd)
-        def _():
-            remote(
-                bsend.at[1, t], relay.at[slot], b_s.at[1, t], u_r.at[slot], dev(7 - p, xx, mir(cc), cc)
-            ).start()
-
-        @pl.when(jnp.logical_and(even_up, jnp.logical_not(is_self)))
-        def _():
-            remote(
-                bsend.at[1, t],
-                brecv.at[1, slot],
-                b_s.at[1, t],
-                b_r.at[1, slot],
-                dev(8 - p, xx, mir(cc), cc),
-            ).start()
-
-        @pl.when(is_self)
-        def _():
-            pltpu.make_async_copy(bsend.at[1, t], brecv.at[1, slot], b_r.at[1, slot]).start()
-
-    loop(0, 8, finish)
+            to = dev(p - 1, xx, zh, cc)
+            remote(bsend.at[0, t], brecv.at[0, slot], b_s.at[0, t], b_r.at[0, slot], to).start()
+
+    loop(0, 8, send_back)
 
     here(rs_s.at[0], rs_r.at[0], rsf_r.at[low]).wait_recv()
     rsn_s[0, 0:HALF, :] = (part[0, 0:HALF, :] + rsf_r[0:HALF, :].astype(F32)).astype(BF16)
@@ -509,15 +512,9 @@
     rsn_s[1, MOST:BLK, :] = (part[1, MOST - HALF : HALF, :] + rsf_r[MOST:BLK, :].astype(F32)).astype(BF16)
     send_rs(rsn_s.at[1, fourth], rsn_r.at[1, fourth], 6, zm)
 
+    loop(0, 8, pass_on)
+
     weight_grad(zh, to_own)
-
-    def pass_on(t):
-        here(u_s.at[t], u_r.at[t], relay.at[t]).wait_recv()
-        remote(relay.at[t], brecv.at[1, t], u_s.at[t], b_r.at[1, t], dev(p + 1, x, zh, c)).start()
-
-    @pl.when(even)
-    def _():
-        loop(0, 8, pass_on)
 
     near = ((3, 0, fourth), (4, 1, low), (5, 0, low), (6, 1, fourth), (7, 0, third), (8, 1, third))
     for i, side, piece in near:
@@ -525,13 +522,15 @@
     wg = own[...] + rsn_r[0].astype(F32) + rsn_r[1].astype(F32)
     wk_out[...] = wg[:, 0:KVW]
     wv_out[...] = wg[:, KVW:KW]
-    gg = gpart[zh]
+    gg = gsum[zh]
     for j in (1, 2, 3):
         here(gg_ss.at[j], gg_rs.at[j], gg_r.at[j]).wait_recv()
         gg = gg + gg_r[j]
     gg_out[...] = jnp.sum(gg, axis=0, keepdims=True)
 
-    def wait_back(t):
+    def take_back(j):
+        t = lax.rem(slot - j + 8, 8)
+
         @pl.when(back_down)
         def _():
             here(b_s.at[0, t], b_r.at[0, t], brecv.at[0, t]).wait_recv()
@@ -540,14 +539,15 @@
         def _():
             here(b_s.at[1, t], b_r.at[1, t], brecv.at[1, t]).wait_recv()
 
-    loop(0, 8, wait_back)
-    for j in range(32):
-        t = (j // 8) * 2 + j % 2
-        b = (j // 2) % 4
-        down = brecv[0, t, b].astype(F32)
-        up = brecv[1, t, b].astype(F32)
-        passed_out[0, :, j * BLK : (j + 1) * BLK] = jnp.where(swap, up, down).astype(BF16)
-        passed_out[1, :, j * BLK : (j + 1) * BLK] = jnp.where(swap, down, up).astype(BF16)
+        for b in range(4):
+            start = lax.div(t, 2) * (8 * BLK) + b * (2 * BLK) + lax.rem(t, 2) * BLK
+            cols = pl.ds(pl.multiple_of(start, BLK), BLK)
+            down = brecv[0, t, b].astype(F32)
+            up = brecv[1, t, b].astype(F32)
+            passed_out[0, :, cols] = jnp.where(swap, up, down).astype(BF16)
+            passed_out[1, :, cols] = jnp.where(swap, down, up).astype(BF16)
+
+    loop(0, 8, take_back)
 
     def drain(t):
         here(ns_s.at[1, t], ns_r.at[1, t], nsend.at[1, t]).wait_send()
@@ -555,7 +555,8 @@
         @pl.when(t != slot)
         def _():
             here(ns_s.at[0, t], ns_r.at[0, t], nsend.at[0, t]).wait_send()
-            here(c_ss.at[t], c_rs.at[t], c_s).wait_send()
+            for e in range(2):
+                here(c_ss.at[e, t], c_rs.at[e, t], c_s.at[e]).wait_send()
 
         @pl.when(even)
         def _():
@@ -586,6 +587,26 @@
     for i, side, piece in near:
         here(rs_s.at[i], rs_r.at[i], rsn_s.at[side, piece]).wait_send()
     store_qg.wait()
+
+
+def deliver(qg, passed, wk, wv, gg, qg_out, passed_out, wk_out, wv_out, gg_out, sem):
+    copies = [
+        pltpu.make_async_copy(wk, wk_out, sem.at[0]),
+        pltpu.make_async_copy(wv, wv_out, sem.at[1]),
+        pltpu.make_async_copy(gg, gg_out, sem.at[2]),
+    ]
+    for m in range(2):
+        for h in range(2):
+            rows = pl.ds(h * (SEQ // 2), SEQ // 2)
+            i = 3 + 4 * m + 2 * h
+            copies.append(
+                pltpu.make_async_copy(passed.at[m, rows], passed_out.at[m, rows], sem.at[i])
+            )
+            copies.append(pltpu.make_async_copy(qg.at[m, rows], qg_out.at[m, rows], sem.at[i + 1]))
+    for copy in copies:
+        copy.start()
+    for copy in copies:
+        copy.wait()
 
 
 def on_device(
@@ -627,10 +648,11 @@
         pltpu.VMEM((2, BLK, KW), BF16),
         pltpu.VMEM((2, 8, 4, SEQ, BLK), BF16),
         pltpu.VMEM((2, 8 * SEQ, 128), F32),
+        pltpu.VMEM((2, 4, 8, BLK), F32),
         pltpu.VMEM((4, 8, BLK), F32),
         pltpu.VMEM((4, 8, BLK), F32),
-        pltpu.VMEM((8, 128), F32),
-        pltpu.VMEM((8, 8, 128), F32),
+        pltpu.VMEM((2, 8, 128), F32),
+        pltpu.VMEM((2, 8, 8, 128), F32),
         pltpu.VMEM((2, 8, SEQ, 128), F32),
         pltpu.VMEM((2, 8, 4, SEQ, BLK), BF16),
         pltpu.VMEM((2, 8, 4, SEQ, BLK), BF16),
@@ -652,23 +674,24 @@
         dma((9,)),
         dma((4,)),
         dma((4,)),
-        dma((8,)),
-        dma((8,)),
+        dma((2, 8)),
+        dma((2, 8)),
         dma((2, 8)),
         dma((2, 8)),
         dma((8,)),
         dma((8,)),
     ]
-    qg, passed, wk, wv, gg = pl.pallas_call(
+    shapes = (
+        jax.ShapeDtypeStruct((2, SEQ, QW), BF16),
+        jax.ShapeDtypeStruct((2, SEQ, D), BF16),
+        jax.ShapeDtypeStruct((BLK, KVW), F32),
+        jax.ShapeDtypeStruct((BLK, KVW), F32),
+        jax.ShapeDtypeStruct((1, BLK), F32),
+    )
+    results = pl.pallas_call(
         kernel,
         name="relay",
-        out_shape=(
-            jax.ShapeDtypeStruct((2, SEQ, QW), BF16),
-            jax.ShapeDtypeStruct((2, SEQ, D), BF16),
-            jax.ShapeDtypeStruct((BLK, KVW), F32),
-            jax.ShapeDtypeStruct((BLK, KVW), F32),
-            jax.ShapeDtypeStruct((1, BLK), F32),
-        ),
+        out_shape=shapes,
         in_specs=[smem, vmem, vmem, vmem, vmem, hbm, hbm, hbm, hbm, hbm],
         out_specs=(hbm, vmem, vmem, vmem, vmem),
         scratch_shapes=scratch,
@@ -687,6 +710,14 @@
         key_weight[0],
         value_weight[0],
     )
+    qg, passed, wk, wv, gg = pl.pallas_call(
+        deliver,
+        name="deliver",
+        out_shape=shapes,
+        in_specs=[vmem] * 5,
+        out_specs=(hbm,) * 5,
+        scratch_shapes=[dma((11,))],
+    )(*results)
     return qg[:, None], passed[:, None], wk[None], wv[None], gg
 
 

time: 140 us -> 129 us (0.921)
  the two profiles are of different devices: /device:TPU:30 before, /device:TPU:1 now
where the time goes in v3:
time: 129 us
  Pallas kernels  128 us (99%)
    pallas_call x1, Pallas kernels, on_device(): pl.pallas_call(kernel, name='relay', out_shape=shapes, in_specs=[smem, vm...  124 us
    pallas_call x1, Pallas kernels, on_device(): pl.pallas_call(deliver, name='deliver', out_shape=shapes, in_specs=[vmem]...  4.24 us

profile of v3, /device:TPU:1, one launch (start us, length us, event | category | flops | bytes accessed | tf_op | source)
XLA Modules:
  0.0 129.1 jit_solution(9234370505099265320)
XLA Ops:
  0.6 124.2 %relay.1 = (bf16[2,64,4096]{2,1,0:T(8,128)(2,1)}, bf16[2,64,8192]{2,1,0:T(8,128)(2,1)}, f32[256,512]{1,0:T(8,128)}, f32[256,512]{1,0:T(8,128)}, f32[1,256]{1,0:T(1,128)}) custom-call(s32[2]{0:T(128)} %flag.1, s32[2,1,64]{2,1,0:T(1,128)} %pos.1, bf16[2,64,512]{2,1,0:T(8,128)(2,1)} %bitcast.20, bf16[2,64,512]{2,1,0:T(8,128)(2,1)} %bitcast.21, ...), custom_call_target="tpu_custom_call" | custom-call | tf_op jit(solution)/shard_map/relay/pallas_call | solution.py:691
  124.9 4.2 %deliver.1 = (bf16[2,64,4096]{2,1,0:T(8,128)(2,1)}, bf16[2,64,8192]{2,1,0:T(8,128)(2,1)}, f32[256,512]{1,0:T(8,128)}, f32[256,512]{1,0:T(8,128)}, f32[1,256]{1,0:T(1,128)}) custom-call(bf16[2,64,4096]{2,1,0:T(8,128)(2,1)} %get-tuple-element.15.qg, bf16[2,64,8192]{2,1,0:T(8,128)(2,1)} %get-tuple-element.16.passed, f32[256,512]{1,0:T(8,128)} %get-tuple-element.17.wk, ...), custom_call_target="tpu_custom_call" | custom-call | tf_op jit(solution)/shard_map/deliver/pallas_call | solution.py:713

commit v4 on v3

--- a/solution.py
+++ b/solution.py
@@ -589,24 +589,22 @@
     store_qg.wait()
 
 
-def deliver(qg, passed, wk, wv, gg, qg_out, passed_out, wk_out, wv_out, gg_out, sem):
-    copies = [
-        pltpu.make_async_copy(wk, wk_out, sem.at[0]),
-        pltpu.make_async_copy(wv, wv_out, sem.at[1]),
-        pltpu.make_async_copy(gg, gg_out, sem.at[2]),
-    ]
+def deliver(qg, passed, wk, wv, gg, qg_out, passed_out, wk_out, wv_out, gg_out, vq, vp, vk, vv, vg, take, give):
+    moves = [(gg, vg, gg_out), (wk, vk, wk_out), (wv, vv, wv_out)]
     for m in range(2):
+        moves.append((qg.at[m], vq.at[m], qg_out.at[m]))
         for h in range(2):
             rows = pl.ds(h * (SEQ // 2), SEQ // 2)
-            i = 3 + 4 * m + 2 * h
-            copies.append(
-                pltpu.make_async_copy(passed.at[m, rows], passed_out.at[m, rows], sem.at[i])
-            )
-            copies.append(pltpu.make_async_copy(qg.at[m, rows], qg_out.at[m, rows], sem.at[i + 1]))
-    for copy in copies:
-        copy.start()
-    for copy in copies:
-        copy.wait()
+            moves.append((passed.at[m, rows], vp.at[m, rows], passed_out.at[m, rows]))
+    loads = [pltpu.make_async_copy(a, v, take.at[i]) for i, (a, v, _) in enumerate(moves)]
+    stores = [pltpu.make_async_copy(v, b, give.at[i]) for i, (_, v, b) in enumerate(moves)]
+    for load in loads:
+        load.start()
+    for load, store in zip(loads, stores):
+        load.wait()
+        store.start()
+    for store in stores:
+        store.wait()
 
 
 def on_device(
@@ -714,9 +712,9 @@
         deliver,
         name="deliver",
         out_shape=shapes,
-        in_specs=[vmem] * 5,
+        in_specs=[hbm] * 5,
         out_specs=(hbm,) * 5,
-        scratch_shapes=[dma((11,))],
+        scratch_shapes=[pltpu.VMEM(t.shape, t.dtype) for t in shapes] + [dma((9,)), dma((9,))],
     )(*results)
     return qg[:, None], passed[:, None], wk[None], wv[None], gg
 

time: 129 us -> 129 us (level)
  no operation moved by 1% of the time
where the time goes in v4:
time: 129 us
  Pallas kernels  128 us (99%)
    pallas_call x1, Pallas kernels, on_device(): pl.pallas_call(kernel, name='relay', out_shape=shapes, in_specs=[smem, vm...  124 us
    pallas_call x1, Pallas kernels, on_device(): pl.pallas_call(deliver, name='deliver', out_shape=shapes, in_specs=[hbm]...  3.63 us

profile of v4, /device:TPU:1, one launch (start us, length us, event | category | flops | bytes accessed | tf_op | source)
XLA Modules:
  0.0 128.5 jit_solution(10550388836923437399)
XLA Ops:
  0.6 124.2 %relay.1 = (bf16[2,64,4096]{2,1,0:T(8,128)(2,1)}, bf16[2,64,8192]{2,1,0:T(8,128)(2,1)}, f32[256,512]{1,0:T(8,128)}, f32[256,512]{1,0:T(8,128)}, f32[1,256]{1,0:T(1,128)}) custom-call(s32[2]{0:T(128)} %flag.1, s32[2,1,64]{2,1,0:T(1,128)} %pos.1, bf16[2,64,512]{2,1,0:T(8,128)(2,1)} %bitcast.20, bf16[2,64,512]{2,1,0:T(8,128)(2,1)} %bitcast.21, ...), custom_call_target="tpu_custom_call" | custom-call | tf_op jit(solution)/shard_map/relay/pallas_call | solution.py:689
  124.9 3.6 %deliver.1 = (bf16[2,64,4096]{2,1,0:T(8,128)(2,1)}, bf16[2,64,8192]{2,1,0:T(8,128)(2,1)}, f32[256,512]{1,0:T(8,128)}, f32[256,512]{1,0:T(8,128)}, f32[1,256]{1,0:T(1,128)}) custom-call(bf16[2,64,4096]{2,1,0:T(8,128)(2,1)} %get-tuple-element.15.qg, bf16[2,64,8192]{2,1,0:T(8,128)(2,1)} %get-tuple-element.16.passed, f32[256,512]{1,0:T(8,128)} %get-tuple-element.17.wk, ...), custom_call_target="tpu_custom_call" | custom-call | tf_op jit(solution)/shard_map/deliver/pallas_call | solution.py:711
